TPU v7x, 256 devices: a whole 4x4x8 slice. The times are simulated.
256 devices in a mesh: ctx: 64 (over x, z, core), fsdp: 4 (over y).
Axes of the slice: x: 4, y: 4, z: 8, core: 2. Of those that a mesh axis runs over, the one named last changes fastest.
Arguments:
- query_rows: bfloat16 [8192, 2560], P('ctx', 'fsdp'), may hold values from -100 to 100
- key_rows: bfloat16 [8192, 512], P('ctx', 'fsdp'), may hold values from -4.5 to 4.5
- value_rows: bfloat16 [8192, 512], P('ctx', 'fsdp'), may hold values from -6 to 6
- mixed_grad: bfloat16 [8192, 2560], P('ctx', 'fsdp'), may hold values from -16 to 16
- layer_grad: bfloat16 [8192, 5120], P('ctx'), may hold values from -16 to 16
- state_feed: bfloat16 [8192, 4096], P('ctx', 'fsdp'), may hold values from -0.09375 to 0.09375
- write_map: bfloat16 [8192, 1024], P('ctx', 'fsdp'), may hold values from -0.25 to 0.25
- read_map: bfloat16 [8192, 1024], P('ctx', 'fsdp'), may hold values from -0.25 to 0.25
- log_decay: float32 [8192, 64], P('ctx', 'fsdp'), may hold values from -1 to 0
- scan_grad: bfloat16 [8192, 4096], P('ctx', 'fsdp'), may hold values from -6 to 6
Outputs:
- query_grad: bfloat16 [8192, 2560], P('ctx', 'fsdp')
- key_grad: bfloat16 [8192, 512], P('ctx', 'fsdp')
- value_grad: bfloat16 [8192, 512], P('ctx', 'fsdp')
- proj_grad: float32 [5120, 2560], P('ctx', 'fsdp')
- feed_grad: bfloat16 [8192, 4096], P('ctx', 'fsdp')
- write_grad: float32 [8192, 1024], P('ctx', 'fsdp')
- read_grad: float32 [8192, 1024], P('ctx', 'fsdp')
All inputs are finite; a program needn't handle non-finite values.
Results may differ from a plain program's by a relative error of at most 0.023.
Values may be sent and summed in bfloat16 or wider, within the bound.
A program may use at most 256 MiB of HBM per device.

v0:
```python
import jax
import jax.numpy as jnp
from jax import lax
from jax.sharding import PartitionSpec as P

HD = 128
GROUPS = 5
SP = 64
NS = 128


HIGHEST = lax.Precision.HIGHEST
MASKED_SCORE = -1e30


def entering(part, axis, combine, identity, reverse):
    count = lax.axis_size(axis)
    place = lax.axis_index(axis)
    ahead = count - 1 - place if reverse else place
    gathered = jax.tree.map(lambda a: lax.all_gather(a, axis), part)
    state = jax.tree.map(lambda a, e: jnp.zeros_like(a) + jnp.asarray(e, a.dtype), part, identity)

    def one(hop, state):
        source = count - 1 - hop if reverse else hop
        return combine(
            state, jax.tree.map(lambda a: lax.dynamic_index_in_dim(a, source, 0, False), gathered)
        )

    return lax.fori_loop(0, ahead, one, state)


def chain_link(earlier, later):
    return (earlier[0] * later[0], later[0][:, None, None] * earlier[1] + later[1])


def per_device(
    query_rows,
    key_rows,
    value_rows,
    mixed_grad,
    layer_grad,
    state_feed,
    write_map,
    read_map,
    log_decay,
    scan_grad,
):
    tokens = query_rows.shape[0]
    kv_heads = key_rows.shape[1] // HD
    score_scale = HD ** (-0.5)
    first_row = lax.axis_index("ctx") * tokens
    query_heads = query_rows.reshape(tokens, kv_heads, GROUPS, HD)
    grad_heads = mixed_grad.reshape(tokens, kv_heads, GROUPS, HD)
    all_keys, all_values = (
        lax.all_gather(key_rows, "ctx", axis=0, tiled=True),
        lax.all_gather(value_rows, "ctx", axis=0, tiled=True),
    )
    key_count = all_keys.shape[0]
    block_rows = min(512, key_count)
    key_heads = all_keys.reshape(key_count, kv_heads, HD)
    value_heads = all_values.reshape(key_count, kv_heads, HD)
    query_pos = first_row + jnp.arange(tokens, dtype=jnp.int32)
    live_blocks = (first_row + tokens + block_rows - 1) // block_rows

    def block_scores(anchor, extent):
        key_block = lax.dynamic_slice_in_dim(key_heads, anchor, extent, 0)
        value_block = lax.dynamic_slice_in_dim(value_heads, anchor, extent, 0)
        key_pos = anchor + jnp.arange(extent, dtype=jnp.int32)
        causal = key_pos[None, :] <= query_pos[:, None]
        scores = (
            jnp.einsum("tkgd,skd->kgts", query_heads, key_block, preferred_element_type=jnp.float32)
            * score_scale
        )
        return (key_block, value_block, causal, jnp.where(causal, scores, MASKED_SCORE))

    def stats_step(block_index, state_carry):
        row_top, summed = state_carry
        key_block, value_block, causal, scores = block_scores(block_index * block_rows, block_rows)
        new_top = jnp.maximum(row_top, jnp.max(scores, axis=-1))
        shrink = jnp.exp(row_top - new_top)
        fresh = jnp.where(causal, jnp.exp(scores - new_top[..., None]), 0.0)
        return (new_top, summed * shrink + jnp.sum(fresh, axis=-1))

    start_state = (
        jnp.full((kv_heads, GROUPS, tokens), MASKED_SCORE, jnp.float32),
        jnp.zeros((kv_heads, GROUPS, tokens), jnp.float32),
    )
    row_top, summed = lax.fori_loop(0, live_blocks, stats_step, start_state)
    log_total = row_top + jnp.log(summed)

    def output_step(block_index, weighted):
        key_block, value_block, causal, scores = block_scores(block_index * block_rows, block_rows)
        weights16 = jnp.where(causal, jnp.exp(scores - log_total[..., None]), 0.0).astype(
            jnp.bfloat16
        )
        return weighted + jnp.einsum(
            "kgts,skd->kgtd", weights16, value_block, preferred_element_type=jnp.float32
        )

    attn_out = lax.fori_loop(
        0, live_blocks, output_step, jnp.zeros((kv_heads, GROUPS, tokens, HD), jnp.float32)
    )
    row_delta = jnp.einsum(
        "tkgd,kgtd->kgt", grad_heads.astype(jnp.float32), attn_out, precision=HIGHEST
    )
    mixed_out = (
        jnp.transpose(attn_out, (2, 0, 1, 3))
        .reshape(tokens, kv_heads * GROUPS * HD)
        .astype(jnp.bfloat16)
    )

    def block_terms(anchor, extent):
        key_block, value_block, causal, scores = block_scores(anchor, extent)
        weights = jnp.where(causal, jnp.exp(scores - log_total[..., None]), 0.0)
        dweights = jnp.einsum(
            "tkgd,skd->kgts", grad_heads, value_block, preferred_element_type=jnp.float32
        )
        dscores = (weights * (dweights - row_delta[..., None])).astype(jnp.bfloat16)
        return (key_block, weights.astype(jnp.bfloat16), dscores)

    def query_terms(key_block, dscores):
        return (
            jnp.einsum("kgts,skd->tkgd", dscores, key_block, preferred_element_type=jnp.float32)
            * score_scale
        )

    def pair_terms(weights16, dscores, extent):
        key_part = (
            jnp.einsum("kgts,tkgd->skd", dscores, query_heads, preferred_element_type=jnp.float32)
            * score_scale
        )
        value_part = jnp.einsum(
            "kgts,tkgd->skd", weights16, grad_heads, preferred_element_type=jnp.float32
        )
        return jnp.stack(
            [key_part.reshape(extent, kv_heads * HD), value_part.reshape(extent, kv_heads * HD)],
            axis=1,
        )

    query_zero = jnp.zeros((tokens, kv_heads, GROUPS, HD), jnp.float32)

    def backward_step(block_index, state_carry):
        query_acc, pair_acc = state_carry
        anchor = block_index * block_rows
        key_block, weights16, dscores = block_terms(anchor, block_rows)
        query_acc = query_acc + query_terms(key_block, dscores)
        current = lax.dynamic_slice_in_dim(pair_acc, anchor, block_rows, 0)
        pair_acc = lax.dynamic_update_slice_in_dim(
            pair_acc, current + pair_terms(weights16, dscores, block_rows), anchor, 0
        )
        return (query_acc, pair_acc)

    pair_zero = jnp.zeros((key_count, 2, kv_heads * HD), jnp.float32)
    query_acc, pair_acc = lax.fori_loop(0, live_blocks, backward_step, (query_zero, pair_zero))
    pair_grad = lax.psum_scatter(pair_acc, "ctx", scatter_dimension=0, tiled=True)
    query_grad = query_acc.reshape(tokens, kv_heads * GROUPS * HD).astype(jnp.bfloat16)
    key_grad = pair_grad[:, 0, :].astype(jnp.bfloat16)
    value_grad = pair_grad[:, 1, :].astype(jnp.bfloat16)
    proj_grad = lax.psum_scatter(
        lax.dot_general(
            layer_grad, mixed_out, (((0,), (0,)), ((), ())), preferred_element_type=jnp.float32
        ),
        "ctx",
        scatter_dimension=0,
        tiled=True,
    )
    ssm_heads = log_decay.shape[1]
    local_groups = write_map.shape[1] // NS
    group_size = ssm_heads // local_groups
    feed_narrow = state_feed.reshape(tokens, ssm_heads, SP)
    grad_narrow = scan_grad.reshape(tokens, ssm_heads, SP)
    write_narrow = jnp.repeat(write_map.reshape(tokens, local_groups, NS), group_size, axis=1)
    read_narrow = jnp.repeat(read_map.reshape(tokens, local_groups, NS), group_size, axis=1)
    feed_rows = feed_narrow.astype(jnp.float32)
    grad_rows = grad_narrow.astype(jnp.float32)
    write_heads = write_narrow.astype(jnp.float32)
    read_heads = read_narrow.astype(jnp.float32)
    running = jnp.cumsum(log_decay, axis=0)
    block_decay = running[-1]
    positions = jnp.arange(tokens, dtype=jnp.int32)
    earlier_mask = (positions[:, None] >= positions[None, :])[None]
    flipped = jnp.transpose(running)
    log_gaps = flipped[:, :, None] - flipped[:, None, :]
    decays = jnp.where(earlier_mask, jnp.exp(jnp.where(earlier_mask, log_gaps, 0.0)), 0.0)
    tail_decay = jnp.exp(block_decay[None, :] - running)
    head_decay = jnp.exp(running)
    local_state = jnp.einsum(
        "sh,shn,shp->hnp", tail_decay, write_heads, feed_rows, precision=HIGHEST
    )
    local_grad = jnp.einsum("sh,shn,shp->hnp", head_decay, read_heads, grad_rows, precision=HIGHEST)
    carried = jnp.exp(block_decay)
    identity_pair = (jnp.ones_like(carried), jnp.zeros_like(local_state))
    state_in = entering((carried, local_state), "ctx", chain_link, identity_pair, False)[1]
    grad_next = entering((carried, local_grad), "ctx", chain_link, identity_pair, True)[1]
    cross_terms = jnp.einsum(
        "ahp,bhp->hab", grad_narrow, feed_narrow, preferred_element_type=jnp.float32
    )
    inner_terms = decays * cross_terms
    read_term = jnp.einsum(
        "th,hnp,thp->thn", head_decay, state_in, grad_rows, precision=HIGHEST
    ) + jnp.einsum("htb,bhn->thn", inner_terms, write_heads, precision=HIGHEST)
    write_term = jnp.einsum(
        "hat,ahn->thn", inner_terms, read_heads, precision=HIGHEST
    ) + jnp.einsum("th,hnp,thp->thn", tail_decay, grad_next, feed_rows, precision=HIGHEST)
    pairing = jnp.einsum(
        "thn,shn->hts", write_narrow, read_narrow, preferred_element_type=jnp.float32
    )
    feed_full = jnp.einsum(
        "hst,hts,shp->thp", decays, pairing, grad_rows, precision=HIGHEST
    ) + jnp.einsum("th,thn,hnp->thp", tail_decay, write_heads, grad_next, precision=HIGHEST)
    feed_grad = feed_full.reshape(tokens, ssm_heads * SP).astype(jnp.bfloat16)
    read_grad = (
        read_term.reshape(tokens, local_groups, group_size, NS)
        .sum(axis=2)
        .reshape(tokens, local_groups * NS)
    )
    write_grad = (
        write_term.reshape(tokens, local_groups, group_size, NS)
        .sum(axis=2)
        .reshape(tokens, local_groups * NS)
    )
    return (query_grad, key_grad, value_grad, proj_grad, feed_grad, write_grad, read_grad)


def solution(mesh):
    return jax.shard_map(
        per_device,
        mesh=mesh,
        in_specs=(
            P("ctx", "fsdp"),
            P("ctx", "fsdp"),
            P("ctx", "fsdp"),
            P("ctx", "fsdp"),
            P("ctx", None),
            P("ctx", "fsdp"),
            P("ctx", "fsdp"),
            P("ctx", "fsdp"),
            P("ctx", "fsdp"),
            P("ctx", "fsdp"),
        ),
        out_specs=(
            P("ctx", "fsdp"),
            P("ctx", "fsdp"),
            P("ctx", "fsdp"),
            P("ctx", "fsdp"),
            P("ctx", "fsdp"),
            P("ctx", "fsdp"),
            P("ctx", "fsdp"),
        ),
        check_vma=False,
    )
```

profile of v0, /device:TPU:1, one launch (start us, length us, event | category | flops | bytes accessed | tf_op | source)
XLA Modules:
  0.0 911.7 jit_solution(2215136721172849700)
XLA Ops:
  11.2 81.0 %all-gather.8.cloned.1.call-done = bf16[8192,128]{1,0:T(8,128)(2,1)} async-done(((bf16[128,128]{1,0:T(8,128)(2,1)}), bf16[8192,128]{1,0:T(8,128)(2,1)}) %all-gather.8.cloned.1.call-update) | async-done | bytes 2097168 | tf_op jit(solution)/shard_map/all_gather | solution.py:55
  92.3 1.7 while.65
  92.4 1.3 fusion.109
  94.0 76.0 %all-gather.10.cloned.1.call-done = bf16[8192,128]{1,0:T(8,128)(2,1)} async-done(((bf16[128,128]{1,0:T(8,128)(2,1)}), bf16[8192,128]{1,0:T(8,128)(2,1)}) %all-gather.10.cloned.1.call-update) | async-done | bytes 2097168 | tf_op jit(solution)/shard_map/all_gather | solution.py:56
  170.0 1.9 while.66
  170.2 1.7 fusion.113
  172.2 3.9 broadcast_in_dim.94
  176.1 6.6 while.67
  176.3 1.4 exponential_select_fusion.3
  177.7 1.2 fusion.124
  178.9 1.2 fusion.125
  180.9 1.9 fusion.127
  184.3 1.3 convolution_bitcast_fusion.8
  186.8 2.3 convolution_bitcast_fusion.7
  189.3 6.6 convolution_bitcast_fusion.4
  195.9 14.0 %copy.150 = f32[5120,640]{1,0:T(8,128)} copy(f32[5120,640]{0,1:T(8,128)} %convolution_bitcast_fusion.4) | data formatting | bytes 26214400
  210.0 164.8 %all-gather.2 = f32[64,1,16]{2,1,0:T(1,128)S(1)} all-gather(f32[1,1,16]{2,1,0:T(1,128)S(1)} %get-tuple-element.570), channel_id=1, replica_groups=mesh['ctx'=64,'fsdp'=4] {'ctx'}, dimensions={0}, use_global_device_ids=true | all-gather | bytes 4160 | tf_op jit(solution)/shard_map/all_gather | solution.py:20
  375.9 2.0 convolution_bitcast_fusion.6
  377.8 1.6 fusion.67
  380.3 73.5 %reduce-scatter.5.cloned.1.call-done = f32[128,2,128]{2,0,1:T(8,128)} async-done(((f32[8192,2,128]{2,0,1:T(8,128)}), f32[128,2,128]{2,0,1:T(8,128)}) %reduce-scatter.5.cloned.1.call-update) | async-done | bytes 131088 | tf_op jit(solution)/shard_map/reduce_scatter | solution.py:155
  455.3 147.3 %all-gather.12.cloned.1.call-done = f32[1024,128,64]{1,2,0:T(8,128)} async-done(((f32[16,128,64]{1,2,0:T(8,128)}), f32[1024,128,64]{1,2,0:T(8,128)}) %all-gather.12.cloned.1.call-update) | async-done | bytes 33554448 | tf_op jit(solution)/shard_map/all_gather | solution.py:20
  602.7 106.9 %while.63 = (s32[]{:T(128)}, f32[16,128,64]{2,1,0:T(8,128)S(1)}, s32[]{:T(128)}, f32[64,16]{1,0:T(8,128)S(1)}, f32[64,16,128,64]{2,3,1,0:T(8,128)}, /*index=5*/s32[]{:T(128)}, s32[]{:T(128)}, s32[]{:T(128)}, s32[]{:T(128)}) while((s32[]{:T(128)}, f32[16,128,64]{2,1,0:T(8,128)S(1)}, s32[]{:T(128)}, f32[64,16]{1,0:T(8,128)S(1)}, ...), condition=%wide.region_12.13_spmd, body=%wide.region_11.12_spmd.sunk | while | flops 262150 | bytes 3670363 | solution.py:29
  604.6 1.1 constant_dynamic-slice_fusion.4
  608.0 1.1 constant_dynamic-slice_fusion.4
  611.4 1.1 constant_dynamic-slice_fusion.4
  613.1 1.1 constant_dynamic-slice_fusion.4
  614.9 1.1 constant_dynamic-slice_fusion.4
  618.3 1.1 constant_dynamic-slice_fusion.4
  621.7 1.1 constant_dynamic-slice_fusion.4
  625.1 1.1 constant_dynamic-slice_fusion.4
  626.8 1.1 constant_dynamic-slice_fusion.4
  628.5 1.1 constant_dynamic-slice_fusion.4
  630.3 1.1 constant_dynamic-slice_fusion.4
  632.0 1.1 constant_dynamic-slice_fusion.4
  635.4 1.1 constant_dynamic-slice_fusion.4
  637.1 1.1 constant_dynamic-slice_fusion.4
  638.8 1.1 constant_dynamic-slice_fusion.4
  640.5 1.1 constant_dynamic-slice_fusion.4
  655.9 1.2 constant_dynamic-slice_fusion.4
  657.7 1.1 constant_dynamic-slice_fusion.4
  662.9 1.1 constant_dynamic-slice_fusion.4
  664.6 1.1 constant_dynamic-slice_fusion.4
  666.3 1.1 constant_dynamic-slice_fusion.4
  671.4 1.1 constant_dynamic-slice_fusion.4
  676.6 1.1 constant_dynamic-slice_fusion.4
  678.3 1.1 constant_dynamic-slice_fusion.4
  681.7 1.2 constant_dynamic-slice_fusion.4
  683.6 1.1 constant_dynamic-slice_fusion.4
  688.7 1.1 constant_dynamic-slice_fusion.4
  690.5 1.1 constant_dynamic-slice_fusion.4
  692.2 1.1 constant_dynamic-slice_fusion.4
  693.9 1.2 constant_dynamic-slice_fusion.4
  699.1 1.1 constant_dynamic-slice_fusion.4
  700.9 1.1 constant_dynamic-slice_fusion.4
  704.3 1.2 constant_dynamic-slice_fusion.4
  706.1 1.1 constant_dynamic-slice_fusion.4
  707.9 1.1 constant_dynamic-slice_fusion.4
  709.6 2.2 fusion.60
  712.7 1.9 bitcast_reduce_fusion.1
  715.5 29.5 %all-gather.14.cloned.1.call-done = f32[1024,128,64]{1,2,0:T(8,128)} async-done(((f32[16,128,64]{1,2,0:T(8,128)}), f32[1024,128,64]{1,2,0:T(8,128)}) %all-gather.14.cloned.1.call-update) | async-done | bytes 33554448 | tf_op jit(solution)/shard_map/all_gather | solution.py:20
  745.1 2.4 while.64
  745.1 1.1 constant_dynamic-slice_fusion.5
  747.5 1.9 fusion.61
  751.3 153.5 %reduce-scatter.7.cloned.1.call-done = f32[80,640]{1,0:T(8,128)} async-done(((f32[5120,640]{1,0:T(8,128)}), f32[80,640]{1,0:T(8,128)}) %reduce-scatter.7.cloned.1.call-update) | async-done | bytes 204816
  (313 shorter events, 81.4 us)
Async XLA Ops:
  7.2 182.1 %copy-start = (bf16[128,5120]{1,0:T(8,128)(2,1)S(1)}, bf16[128,5120]{1,0:T(8,128)(2,1)}, u32[]{:S(2)}) copy-start(bf16[128,5120]{1,0:T(8,128)(2,1)} %param.24) | copy-start | bytes 3932164
  7.2 85.1 %all-gather.8.cloned.1.call-start = ((), (), s32[]{:S(2)}) async-start(), calls=%async_computation.2 | async-start | bytes 2129920 | tf_op jit(solution)/shard_map/all_gather | solution.py:55
  7.9 162.1 %all-gather.10.cloned.1.call-start = ((), (), s32[]{:S(2)}) async-start(), calls=%async_computation.3 | async-start | bytes 2129920 | tf_op jit(solution)/shard_map/all_gather | solution.py:56
  8.7 445.1 %reduce-scatter.5.cloned.1.call-start = ((), (), s32[]{:S(2)}) async-start(), calls=%async_computation.4 | async-start | bytes 8519680 | tf_op jit(solution)/shard_map/reduce_scatter | solution.py:155
  182.8 0.7 copy-start.14
  182.8 1.0 copy-start.9
  182.8 1.4 copy-start.11
  182.8 419.8 %all-gather.12.cloned.1.call-start = ((), (), s32[]{:S(2)}) async-start(), calls=%async_computation.5 | async-start | bytes 34078720 | tf_op jit(solution)/shard_map/all_gather | solution.py:20
  183.9 192.0 %copy-start.2 = (bf16[128,1024]{0,1:T(8,128)(2,1)}, bf16[128,1024]{0,1:T(8,128)(2,1)S(1)}, u32[]{:S(2)}) copy-start(bf16[128,1024]{0,1:T(8,128)(2,1)S(1)} %copy.117) | copy-start | bytes 786436
  184.2 1.6 copy-start.10
  184.3 2.3 copy-start.12
  185.7 559.3 %all-gather.14.cloned.1.call-start = ((), (), s32[]{:S(2)}) async-start(), calls=%async_computation.6 | async-start | bytes 34078720 | tf_op jit(solution)/shard_map/all_gather | solution.py:20
  189.1 715.7 %reduce-scatter.7.cloned.1.call-start = ((), (), s32[]{:S(2)}) async-start(), calls=%async_computation.7 | async-start | bytes 13312000
  209.9 164.9 %copy-start.7 = (bf16[128,1024]{0,1:T(8,128)(2,1)S(1)}, bf16[128,1024]{0,1:T(8,128)(2,1)}, u32[]{:S(2)}) copy-start(bf16[128,1024]{0,1:T(8,128)(2,1)} %copy.122) | copy-start | bytes 786436
  375.3 2.5 copy-start.4
  709.6 3.1 copy-start.13
  709.6 3.1 copy-start.6
  709.6 3.1 copy-start.8
  745.1 2.5 copy-start.3
  747.5 1.9 copy-start.5
  747.5 157.3 %copy-start.1 = (bf16[128,5120]{1,0:T(8,128)(2,1)S(1)}, bf16[128,5120]{1,0:T(8,128)(2,1)}, u32[]{:S(2)}) copy-start(bf16[128,5120]{1,0:T(8,128)(2,1)} %param.24) | copy-start | bytes 3932164
Sparse Core Ops, SparseCore 0:
  10.8 81.4 all-gather.7
  95.0 74.9 all-gather.9
  182.9 270.7 reduce-scatter.4
  456.7 145.8 all-gather.11
  605.6 139.3 all-gather.13
  750.3 154.4 reduce-scatter.6
where the time goes:
time: 923 us; the launch traced here: 912 us
  waiting for transfers between devices  562 us (61%)
  blocking collectives  165 us (18%)
  local copies, waits for them, and re-layouts  120 us (13%)
  matrix products  29.4 us (3%)
  other arithmetic  17.5 us (2%)
  between operations  14.4 us (2%)
    all_gather x2, waiting for transfers between devices, entering(): gathered = jax.tree.map(lambda a: lax.all_gather(a, axis), part)  177 us
    all_gather x1, blocking collectives, entering(): gathered = jax.tree.map(lambda a: lax.all_gather(a, axis), part)  165 us
    unnamed x7, waiting for transfers between devices  155 us
    dynamic_slice x126, local copies, waits for them, and re-layouts, one(): lax.dynamic_index_in_dim(a, source, 0, False)  90.7 us
    all_gather x1, waiting for transfers between devices, per_device(): lax.all_gather(key_rows, 'ctx', axis=0, tiled=True)  81 us
    all_gather x1, waiting for transfers between devices, per_device(): lax.all_gather(value_rows, 'ctx', axis=0, tiled=True)  76 us
    reduce_scatter x1, waiting for transfers between devices, per_device(): lax.psum_scatter(pair_acc, 'ctx', scatter_dimension=0, tiled=True)  73.5 us
    unnamed x43, local copies, waits for them, and re-layouts  21.9 us
  transfers between devices with their start and end apart: 6, of which 6 were waited for; matrix products, arithmetic and copies ran while one was open for 17% of the time, Pallas kernels for 0%

commit v1 on v0

v1 whole, which is shorter than its diff:
```python
import functools
import jax
import jax.numpy as jnp
from jax import lax
from jax.experimental import pallas as pl
from jax.experimental.pallas import tpu as pltpu
from jax.sharding import PartitionSpec as P

HD = 128
SP = 64
NS = 128
GROUPS = 5
ROWS = 128 * GROUPS
TK = 512
SCALE = HD ** (-0.5)
LOG2E = 1.4426950408889634
MESH = pl.DeviceIdType.MESH
F32 = jnp.float32
BF16 = jnp.bfloat16


def dot(a, b, ca, cb):
    return lax.dot_general(a, b, (((ca,), (cb,)), ((), ())), preferred_element_type=F32)


class Place:
    def __init__(self):
        self.me = lax.axis_index("ctx")
        self.y = lax.axis_index("fsdp")
        self.core = self.me % 2
        self.z = (self.me // 2) % 8
        self.x = self.me // 16

    def dev(self, x, z, core):
        return ((x * 8 + z) * 2 + core, self.y)


def add16(a, b):
    return (a.astype(F32) + b.astype(F32)).astype(BF16)


def att_kernel(q_ref, k_ref, v_ref, do_ref, dq_ref, dk_ref, dv_ref, mo_ref,
               kv, dkv, pst, qs, dot_ref, mst, l_ref, acc, sib,
               x1, x2, z1,
               ag_send, ag_recv, sib_recv, rs_send, rs_sib, rs_x, rs_z):
    p = Place()
    me, x, z, core = p.me, p.x, p.z, p.core
    other = 1 - core

    barrier = pltpu.get_barrier_semaphore()

    def greet(i, c):
        t = (me + i) % 64
        pl.semaphore_signal(barrier, inc=1, device_id=(t, p.y), device_id_type=MESH)
        return c

    lax.fori_loop(1, 64, greet, 0)
    kv[core, x, z, 0] = k_ref[...]
    kv[core, x, z, 1] = v_ref[...]
    pl.semaphore_wait(barrier, 63)

    def push(c, bx, bz, half, target):
        if half is None:
            src, sem = kv.at[c, bx, bz], ag_recv.at[bx, bz, 0]
        else:
            src, sem = kv.at[c, bx, bz, half], ag_recv.at[bx, bz, half]
        pltpu.make_async_remote_copy(
            src_ref=src, dst_ref=src, send_sem=ag_send, recv_sem=sem,
            device_id=target, device_id_type=MESH).start()

    def sibling(c, bx, bz):
        pltpu.make_async_remote_copy(
            src_ref=kv.at[c, bx, bz], dst_ref=kv.at[c, bx, bz], send_sem=ag_send,
            recv_sem=sib_recv.at[bx, bz], device_id=p.dev(x, z, 1 - c), device_id_type=MESH).start()

    def got(c, bx, bz, half=None):
        if half is None:
            ref, sem = kv.at[c, bx, bz], ag_recv.at[bx, bz, 0]
        else:
            ref, sem = kv.at[c, bx, bz, half], ag_recv.at[bx, bz, half]
        pltpu.make_async_remote_copy(
            src_ref=ref, dst_ref=ref, send_sem=ag_send, recv_sem=sem,
            device_id=p.dev(x, z, 1 - c), device_id_type=MESH).wait_recv()

    xr, xl, xo = (x + 1) % 4, (x + 3) % 4, (x + 2) % 4

    def zz(s):
        return (z + s + 8) % 8

    @pl.when(core == 0)
    def _():
        right, left = p.dev(x, zz(1), 0), p.dev(x, zz(-1), 0)
        xright, xleft = p.dev(xr, z, 0), p.dev(xl, z, 0)

        def spread(bz):
            push(0, x, bz, None, xright)
            push(0, x, bz, None, xleft)
            sibling(0, x, bz)

        def across(bz):
            got(0, xl, bz)
            push(0, xl, bz, 0, xright)
            sibling(0, xl, bz)
            got(0, xr, bz)
            push(0, xr, bz, 1, xleft)
            sibling(0, xr, bz)

        push(0, x, z, None, right)
        push(0, x, z, None, left)
        spread(z)
        for s in (1, 2, 3):
            got(0, x, zz(-s))
            push(0, x, zz(-s), None if s < 3 else 0, right)
            spread(zz(-s))
            got(0, x, zz(s))
            push(0, x, zz(s), None if s < 3 else 1, left)
            spread(zz(s))
            if s == 1:
                across(z)
            else:
                across(zz(1 - s))
                across(zz(s - 1))
        got(0, x, zz(4), 0)
        got(0, x, zz(4), 1)
        spread(zz(4))
        across(zz(-3))
        across(zz(3))
        across(zz(4))
        for s in (0, 1, -1, 2, -2, 3, -3, 4):
            got(0, xo, zz(s), 0)
            got(0, xo, zz(s), 1)
            sibling(0, xo, zz(s))

    @pl.when(core == 1)
    def _():
        right, left = p.dev(x, zz(1), 1), p.dev(x, zz(-1), 1)
        xright, xleft = p.dev(xr, z, 1), p.dev(xl, z, 1)

        def spread(bx):
            push(1, bx, z, None, right)
            push(1, bx, z, None, left)
            sibling(1, bx, z)

        push(1, x, z, None, xright)
        push(1, x, z, None, xleft)
        spread(x)
        got(1, xl, z)
        push(1, xl, z, 0, xright)
        spread(xl)
        got(1, xr, z)
        push(1, xr, z, 1, xleft)
        spread(xr)

        def along(bx, s):
            got(1, bx, zz(-s))
            push(1, bx, zz(-s), None if s < 3 else 0, right)
            sibling(1, bx, zz(-s))
            got(1, bx, zz(s))
            push(1, bx, zz(s), None if s < 3 else 1, left)
            sibling(1, bx, zz(s))

        along(x, 1)
        got(1, xo, z, 0)
        got(1, xo, z, 1)
        spread(xo)
        along(xl, 1)
        along(xr, 1)
        along(x, 2)
        along(xo, 1)
        along(xl, 2)
        along(xr, 2)
        along(x, 3)
        along(xo, 2)
        along(xl, 3)
        along(xr, 3)
        along(xo, 3)
        for bx in (x, xl, xr, xo):
            got(1, bx, zz(4), 0)
            got(1, bx, zz(4), 1)
            sibling(1, bx, zz(4))

    for g in range(GROUPS):
        cols = pl.ds(g * 128, 128)
        qs[g * 128:(g + 1) * 128, :] = q_ref[:, cols]
        dot_ref[:, cols] = do_ref[:, cols].astype(F32).T

    def zero(i, c):
        dkv[i // 32, (i // 8) % 4, i % 8] = jnp.zeros((2, 128, 128), BF16)
        return c

    lax.fori_loop(0, 64, zero, 0)
    acc[...] = jnp.zeros_like(acc)
    l_ref[...] = jnp.zeros_like(l_ref)

    def sib_wait(i, c):
        bx, bz = i // 8, i % 8
        pltpu.make_async_remote_copy(
            src_ref=kv.at[other, bx, bz], dst_ref=kv.at[other, bx, bz], send_sem=ag_send,
            recv_sem=sib_recv.at[bx, bz], device_id=p.dev(x, z, other), device_id_type=MESH).wait_recv()
        return c

    lax.fori_loop(0, 32, sib_wait, 0)
    whole = kv.at[0]
    part = kv.at[1, pl.ds(0, 3)]
    tail = kv.at[1, 3, pl.ds(0, 7)]
    for ref in (whole, part, tail):
        pltpu.make_async_copy(ref, ref, ag_send).wait()

    diag = me // 4

    def keys(j, which):
        return kv[:, j // 4, pl.ds(2 * (j % 4), 2), which].reshape(TK, HD)

    def forward(j, top, masked):
        s = dot(keys(j, 0), qs[...], 1, 1)
        if masked:
            row = lax.broadcasted_iota(jnp.int32, (TK, ROWS), 0)
            col = lax.broadcasted_iota(jnp.int32, (TK, ROWS), 1)
            pos = ((j * 4 + ((row // 128) % 2) * 2 + row // 256) * 128) + row % 128
            s = jnp.where(pos <= me * 128 + col % 128, s, -1e30)
        new = jnp.maximum(top, jnp.max(s, axis=0, keepdims=True))
        w = jnp.exp2((s - new) * (SCALE * LOG2E))
        shrink = jnp.exp2((top - new) * (SCALE * LOG2E))
        l_ref[...] = l_ref[...] * shrink + jnp.sum(w, axis=0, keepdims=True)
        w16 = w.astype(BF16)
        pst[j] = w16
        mst[j] = new
        acc[...] = acc[...] * shrink + dot(keys(j, 1), w16, 0, 0)
        return new

    top = lax.fori_loop(0, diag, lambda j, t: forward(j, t, False), jnp.full((1, ROWS), -1e30, F32))
    top = forward(diag, top, True)
    inv = 1.0 / l_ref[...]
    out_t = acc[...] * inv
    delta = jnp.sum(out_t * dot_ref[...], axis=0, keepdims=True)
    for g in range(GROUPS):
        mo_ref[:, g * 128:(g + 1) * 128] = out_t[:, g * 128:(g + 1) * 128].T.astype(BF16)
    acc[...] = jnp.zeros_like(acc)

    def backward(j, c):
        factor = jnp.exp2((mst[j] - top) * (SCALE * LOG2E)) * inv
        grad = (dot_ref[...] * factor).astype(BF16)
        dw = dot(keys(j, 1), grad, 1, 0)
        w16 = pst[j]
        ds = (w16.astype(F32) * (dw - delta * factor)).astype(BF16)
        dk = dot(ds, qs[...], 1, 0) * SCALE
        dv = dot(w16, grad, 1, 1)
        acc[...] = acc[...] + dot(keys(j, 0), ds, 0, 0)
        dkv[:, j // 4, pl.ds(2 * (j % 4), 2), 0] = dk.astype(BF16).reshape(2, 2, 128, 128)
        dkv[:, j // 4, pl.ds(2 * (j % 4), 2), 1] = dv.astype(BF16).reshape(2, 2, 128, 128)
        return c

    lax.fori_loop(0, diag + 1, backward, 0)
    for g in range(GROUPS):
        dq_ref[:, g * 128:(g + 1) * 128] = (acc[:, g * 128:(g + 1) * 128] * SCALE).T.astype(BF16)

    def remote(src, dst, sem, target):
        return pltpu.make_async_remote_copy(
            src_ref=src, dst_ref=dst, send_sem=rs_send, recv_sem=sem,
            device_id=target, device_id_type=MESH)

    for i in range(4):
        remote(dkv.at[other, i], sib.at[i], rs_sib.at[i], p.dev(x, z, other)).start()

    def sib_add(i, c):
        remote(dkv.at[other, i], sib.at[i], rs_sib.at[i], p.dev(x, z, other)).wait_recv()

        def one(b, c):
            dkv[core, i, b] = add16(dkv[core, i, b], sib[i, b])
            return c

        return lax.fori_loop(0, 8, one, c)

    lax.fori_loop(0, 4, sib_add, 0)

    @pl.when(core == 0)
    def _():
        xright, xleft = p.dev(xr, z, 0), p.dev(xl, z, 0)
        ra = remote(dkv.at[0, xo, :, 0], x1.at[0], rs_x.at[0, 0], xright)
        la = remote(dkv.at[0, xo, :, 1], x1.at[1], rs_x.at[0, 1], xleft)
        ra.start()
        la.start()
        ra.wait_recv()
        dkv[0, xr, :, 0] = add16(dkv[0, xr, :, 0], x1[0])
        rb = remote(dkv.at[0, xr], x2.at[0], rs_x.at[1, 0], xright)
        rb.start()
        la.wait_recv()
        dkv[0, xl, :, 1] = add16(dkv[0, xl, :, 1], x1[1])
        lb = remote(dkv.at[0, xl], x2.at[1], rs_x.at[1, 1], xleft)
        lb.start()
        rb.wait_recv()
        lb.wait_recv()

        def one(b, c):
            dkv[0, x, b] = (dkv[0, x, b].astype(F32) + x2[0, b].astype(F32) + x2[1, b].astype(F32)).astype(BF16)
            return c

        lax.fori_loop(0, 8, one, 0)
        right, left = p.dev(x, zz(1), 0), p.dev(x, zz(-1), 0)
        ra = remote(dkv.at[0, x, zz(4), 0], z1.at[0, 0, 0, 0], rs_z.at[0, 0], right)
        la = remote(dkv.at[0, x, zz(4), 1], z1.at[1, 0, 0, 1], rs_z.at[0, 1], left)
        ra.start()
        la.start()
        for s in (1, 2, 3):
            d = 4 - s
            ra.wait_recv()
            if s == 1:
                dkv[0, x, zz(d), 0] = add16(dkv[0, x, zz(d), 0], z1[0, 0, 0, 0])
            else:
                dkv[0, x, zz(d)] = add16(dkv[0, x, zz(d)], z1[0, s - 1, 0])
            ra = remote(dkv.at[0, x, zz(d)], z1.at[0, s, 0], rs_z.at[s, 0], right)
            ra.start()
            la.wait_recv()
            if s == 1:
                dkv[0, x, zz(-d), 1] = add16(dkv[0, x, zz(-d), 1], z1[1, 0, 0, 1])
            else:
                dkv[0, x, zz(-d)] = add16(dkv[0, x, zz(-d)], z1[1, s - 1, 0])
            la = remote(dkv.at[0, x, zz(-d)], z1.at[1, s, 0], rs_z.at[s, 1], left)
            la.start()
        ra.wait_recv()
        la.wait_recv()
        for ref, h in ((dk_ref, 0), (dv_ref, 1)):
            ref[...] = (dkv[0, x, z, h].astype(F32) + z1[0, 3, 0, h].astype(F32) + z1[1, 3, 0, h].astype(F32)).astype(BF16)

    @pl.when(core == 1)
    def _():
        right, left = p.dev(x, zz(1), 1), p.dev(x, zz(-1), 1)
        ra = remote(dkv.at[1, :, zz(4), 0], z1.at[0, 0, :, 0], rs_z.at[0, 0], right)
        la = remote(dkv.at[1, :, zz(4), 1], z1.at[1, 0, :, 1], rs_z.at[0, 1], left)
        ra.start()
        la.start()
        for s in (1, 2, 3):
            d = 4 - s
            ra.wait_recv()
            if s == 1:
                dkv[1, :, zz(d), 0] = add16(dkv[1, :, zz(d), 0], z1[0, 0, :, 0])
            else:
                dkv[1, :, zz(d)] = add16(dkv[1, :, zz(d)], z1[0, s - 1])
            ra = remote(dkv.at[1, :, zz(d)], z1.at[0, s], rs_z.at[s, 0], right)
            ra.start()
            la.wait_recv()
            if s == 1:
                dkv[1, :, zz(-d), 1] = add16(dkv[1, :, zz(-d), 1], z1[1, 0, :, 1])
            else:
                dkv[1, :, zz(-d)] = add16(dkv[1, :, zz(-d)], z1[1, s - 1])
            la = remote(dkv.at[1, :, zz(-d)], z1.at[1, s], rs_z.at[s, 1], left)
            la.start()
        ra.wait_recv()
        la.wait_recv()

        def one(b, c):
            dkv[1, b, z] = (dkv[1, b, z].astype(F32) + z1[0, 3, b].astype(F32) + z1[1, 3, b].astype(F32)).astype(BF16)
            return c

        lax.fori_loop(0, 4, one, 0)
        xright, xleft = p.dev(xr, z, 1), p.dev(xl, z, 1)
        ra = remote(dkv.at[1, xo, z, 0], x1.at[0, 0], rs_x.at[0, 0], xright)
        la = remote(dkv.at[1, xo, z, 1], x1.at[1, 0], rs_x.at[0, 1], xleft)
        ra.start()
        la.start()
        ra.wait_recv()
        dkv[1, xr, z, 0] = add16(dkv[1, xr, z, 0], x1[0, 0])
        rb = remote(dkv.at[1, xr, z], x2.at[0, 0], rs_x.at[1, 0], xright)
        rb.start()
        la.wait_recv()
        dkv[1, xl, z, 1] = add16(dkv[1, xl, z, 1], x1[1, 0])
        lb = remote(dkv.at[1, xl, z], x2.at[1, 0], rs_x.at[1, 1], xleft)
        lb.start()
        rb.wait_recv()
        lb.wait_recv()
        for ref, h in ((dk_ref, 0), (dv_ref, 1)):
            ref[...] = (dkv[1, x, z, h].astype(F32) + x2[0, 0, h].astype(F32) + x2[1, 0, h].astype(F32)).astype(BF16)

    for ref in (whole, part, tail):
        pltpu.make_async_copy(ref, ref, rs_send).wait()


def attention(query_rows, key_rows, value_rows, mixed_grad):
    vm = pl.BlockSpec(memory_space=pltpu.VMEM)
    dma = pltpu.SemaphoreType.DMA
    return pl.pallas_call(
        att_kernel,
        out_shape=(
            jax.ShapeDtypeStruct((128, ROWS), BF16),
            jax.ShapeDtypeStruct((128, 128), BF16),
            jax.ShapeDtypeStruct((128, 128), BF16),
            jax.ShapeDtypeStruct((128, ROWS), BF16),
        ),
        in_specs=[vm] * 4,
        out_specs=(vm,) * 4,
        scratch_shapes=[
            pltpu.VMEM((2, 4, 8, 2, 128, 128), BF16),
            pltpu.VMEM((2, 4, 8, 2, 128, 128), BF16),
            pltpu.VMEM((16, TK, ROWS), BF16),
            pltpu.VMEM((ROWS, HD), BF16),
            pltpu.VMEM((HD, ROWS), F32),
            pltpu.VMEM((16, 1, ROWS), F32),
            pltpu.VMEM((1, ROWS), F32),
            pltpu.VMEM((HD, ROWS), F32),
            pltpu.VMEM((4, 8, 2, 128, 128), BF16),
            pltpu.VMEM((2, 8, 128, 128), BF16),
            pltpu.VMEM((2, 8, 2, 128, 128), BF16),
            pltpu.VMEM((2, 4, 4, 2, 128, 128), BF16),
            dma,
            dma((4, 8, 2)),
            dma((4, 8)),
            dma,
            dma((4,)),
            dma((2, 2)),
            dma((4, 2)),
        ],
        compiler_params=pltpu.CompilerParams(
            collective_id=0, has_side_effects=True, vmem_limit_bytes=58 * 2**20
        ),
    )(query_rows, key_rows, value_rows, mixed_grad)


HIGHEST = lax.Precision.HIGHEST


def entering(part, axis, combine, identity, reverse):
    count = lax.axis_size(axis)
    place = lax.axis_index(axis)
    ahead = count - 1 - place if reverse else place
    gathered = jax.tree.map(lambda a: lax.all_gather(a, axis), part)
    state = jax.tree.map(lambda a, e: jnp.zeros_like(a) + jnp.asarray(e, a.dtype), part, identity)

    def one(hop, state):
        source = count - 1 - hop if reverse else hop
        return combine(
            state, jax.tree.map(lambda a: lax.dynamic_index_in_dim(a, source, 0, False), gathered)
        )

    return lax.fori_loop(0, ahead, one, state)


def chain_link(earlier, later):
    return (earlier[0] * later[0], later[0][:, None, None] * earlier[1] + later[1])


def per_device(
    query_rows,
    key_rows,
    value_rows,
    mixed_grad,
    layer_grad,
    state_feed,
    write_map,
    read_map,
    log_decay,
    scan_grad,
):
    tokens = query_rows.shape[0]
    query_grad, key_grad, value_grad, mixed_out = attention(query_rows, key_rows, value_rows, mixed_grad)
    proj_grad = lax.psum_scatter(
        lax.dot_general(
            layer_grad, mixed_out, (((0,), (0,)), ((), ())), preferred_element_type=jnp.float32
        ),
        "ctx",
        scatter_dimension=0,
        tiled=True,
    )
    ssm_heads = log_decay.shape[1]
    local_groups = write_map.shape[1] // NS
    group_size = ssm_heads // local_groups
    feed_narrow = state_feed.reshape(tokens, ssm_heads, SP)
    grad_narrow = scan_grad.reshape(tokens, ssm_heads, SP)
    write_narrow = jnp.repeat(write_map.reshape(tokens, local_groups, NS), group_size, axis=1)
    read_narrow = jnp.repeat(read_map.reshape(tokens, local_groups, NS), group_size, axis=1)
    feed_rows = feed_narrow.astype(jnp.float32)
    grad_rows = grad_narrow.astype(jnp.float32)
    write_heads = write_narrow.astype(jnp.float32)
    read_heads = read_narrow.astype(jnp.float32)
    running = jnp.cumsum(log_decay, axis=0)
    block_decay = running[-1]
    positions = jnp.arange(tokens, dtype=jnp.int32)
    earlier_mask = (positions[:, None] >= positions[None, :])[None]
    flipped = jnp.transpose(running)
    log_gaps = flipped[:, :, None] - flipped[:, None, :]
    decays = jnp.where(earlier_mask, jnp.exp(jnp.where(earlier_mask, log_gaps, 0.0)), 0.0)
    tail_decay = jnp.exp(block_decay[None, :] - running)
    head_decay = jnp.exp(running)
    local_state = jnp.einsum(
        "sh,shn,shp->hnp", tail_decay, write_heads, feed_rows, precision=HIGHEST
    )
    local_grad = jnp.einsum("sh,shn,shp->hnp", head_decay, read_heads, grad_rows, precision=HIGHEST)
    carried = jnp.exp(block_decay)
    identity_pair = (jnp.ones_like(carried), jnp.zeros_like(local_state))
    state_in = entering((carried, local_state), "ctx", chain_link, identity_pair, False)[1]
    grad_next = entering((carried, local_grad), "ctx", chain_link, identity_pair, True)[1]
    cross_terms = jnp.einsum(
        "ahp,bhp->hab", grad_narrow, feed_narrow, preferred_element_type=jnp.float32
    )
    inner_terms = decays * cross_terms
    read_term = jnp.einsum(
        "th,hnp,thp->thn", head_decay, state_in, grad_rows, precision=HIGHEST
    ) + jnp.einsum("htb,bhn->thn", inner_terms, write_heads, precision=HIGHEST)
    write_term = jnp.einsum(
        "hat,ahn->thn", inner_terms, read_heads, precision=HIGHEST
    ) + jnp.einsum("th,hnp,thp->thn", tail_decay, grad_next, feed_rows, precision=HIGHEST)
    pairing = jnp.einsum(
        "thn,shn->hts", write_narrow, read_narrow, preferred_element_type=jnp.float32
    )
    feed_full = jnp.einsum(
        "hst,hts,shp->thp", decays, pairing, grad_rows, precision=HIGHEST
    ) + jnp.einsum("th,thn,hnp->thp", tail_decay, write_heads, grad_next, precision=HIGHEST)
    feed_grad = feed_full.reshape(tokens, ssm_heads * SP).astype(jnp.bfloat16)
    read_grad = (
        read_term.reshape(tokens, local_groups, group_size, NS)
        .sum(axis=2)
        .reshape(tokens, local_groups * NS)
    )
    write_grad = (
        write_term.reshape(tokens, local_groups, group_size, NS)
        .sum(axis=2)
        .reshape(tokens, local_groups * NS)
    )
    return (query_grad, key_grad, value_grad, proj_grad, feed_grad, write_grad, read_grad)


def solution(mesh):
    return jax.shard_map(
        per_device,
        mesh=mesh,
        in_specs=(
            P("ctx", "fsdp"),
            P("ctx", "fsdp"),
            P("ctx", "fsdp"),
            P("ctx", "fsdp"),
            P("ctx", None),
            P("ctx", "fsdp"),
            P("ctx", "fsdp"),
            P("ctx", "fsdp"),
            P("ctx", "fsdp"),
            P("ctx", "fsdp"),
        ),
        out_specs=(
            P("ctx", "fsdp"),
            P("ctx", "fsdp"),
            P("ctx", "fsdp"),
            P("ctx", "fsdp"),
            P("ctx", "fsdp"),
            P("ctx", "fsdp"),
            P("ctx", "fsdp"),
        ),
        check_vma=False,
    )
```

time: 923 us -> 576 us (0.62)
  the two profiles are of different devices: /device:TPU:1 before, /device:TPU:231 now
where the time goes in v1:
time: 576 us; the launch traced here: 569 us
  other arithmetic  152 us (26%)
  local copies, waits for them, and re-layouts  116 us (20%)
  Pallas kernels  114 us (20%)
  waiting for transfers between devices  101 us (18%)
  blocking collectives  45.4 us (8%)
  matrix products  25.5 us (4%)
  between operations  13.9 us (2%)
    add x63, other arithmetic, chain_link(): later[0][:, None, None] * earlier[1] + later[1]  152 us
    pallas_call x1, Pallas kernels, attention(): pl.pallas_call(att_kernel, out_shape=(jax.ShapeDtypeStruct((128, ROWS), B...  114 us
    all_gather x2, waiting for transfers between devices, entering(): gathered = jax.tree.map(lambda a: lax.all_gather(a, axis), part)  101 us
    dynamic_slice x126, local copies, waits for them, and re-layouts, one(): lax.dynamic_index_in_dim(a, source, 0, False)  89.4 us
    all_gather x1, blocking collectives, entering(): gathered = jax.tree.map(lambda a: lax.all_gather(a, axis), part)  45.4 us
    unnamed x26, local copies, waits for them, and re-layouts  22.4 us
  transfers between devices with their start and end apart: 3, of which 1 were waited for; matrix products, arithmetic and copies ran while one was open for 50% of the time, Pallas kernels for 20%

profile of v1, /device:TPU:231, one launch (start us, length us, event | category | flops | bytes accessed | tf_op | source)
XLA Modules:
  0.0 569.4 jit_solution(8672636238828655270)
XLA Ops:
  15.5 114.2 %shard_map.153 = (bf16[128,640]{1,0:T(8,128)(2,1)}, bf16[128,128]{1,0:T(8,128)(2,1)}, bf16[128,128]{1,0:T(8,128)(2,1)}, bf16[128,640]{1,0:T(8,128)(2,1)}) custom-call(bf16[128,640]{1,0:T(8,128)(2,1)} %q_ref.1, bf16[128,128]{1,0:T(8,128)(2,1)} %k_ref.1, bf16[128,128]{1,0:T(8,128)(2,1)} %v_ref.1, bf16[128,640]{1,0:T(8,128)(2,1)} %do_ref.1), custom_call_target="tpu_custom_call" | custom-call | tf_op jit(solution)/shard_map/pallas_call | solution.py:381
  129.8 7.6 %convolution_bitcast_fusion = f32[5120,640]{0,1:T(8,128)} fusion(bf16[128,640]{1,0:T(8,128)(2,1)} %get-tuple-element.142, bf16[128,5120]{1,0:T(8,128)(2,1)S(1)} %copy-done), kind=kOutput, calls=%fused_computation.6 | convolution fusion | flops 838860800 | bytes 14581760 | tf_op jit(solution)/shard_map/dot_general | solution.py:456
  137.3 14.2 %copy.100 = f32[5120,640]{1,0:T(8,128)} copy(f32[5120,640]{0,1:T(8,128)} %convolution_bitcast_fusion) | data formatting | bytes 26214400
  151.6 45.4 %all-gather.2 = f32[64,1,16]{2,1,0:T(1,128)S(1)} all-gather(f32[1,1,16]{2,1,0:T(1,128)S(1)} %get-tuple-element.236), channel_id=1, replica_groups=mesh['ctx'=64,'fsdp'=4] {'ctx'}, dimensions={0}, use_global_device_ids=true | all-gather | bytes 4160 | tf_op jit(solution)/shard_map/all_gather | solution.py:425
  204.9 3.1 bitcast_reduce_fusion.1
  208.9 100.7 %all-gather.8.cloned.1.call-done = f32[1024,128,64]{1,2,0:T(8,128)} async-done(((f32[16,128,64]{1,2,0:T(8,128)}), f32[1024,128,64]{1,2,0:T(8,128)}) %all-gather.8.cloned.1.call-update) | async-done | bytes 33554448 | tf_op jit(solution)/shard_map/all_gather | solution.py:425
  310.7 243.1 %while.27 = (s32[]{:T(128)}, f32[16,128,64]{2,1,0:T(8,128)}, s32[]{:T(128)}, f32[64,16]{1,0:T(8,128)S(1)}, f32[64,16,128,64]{2,3,1,0:T(8,128)}, /*index=5*/s32[]{:T(128)}, s32[]{:T(128)}, s32[]{:T(128)}) while((s32[]{:T(128)}, f32[16,128,64]{2,1,0:T(8,128)}, s32[]{:T(128)}, f32[64,16]{1,0:T(8,128)S(1)}, f32[64,16,128,64]{2,3,1,0:T(8,128)}, ...), condition=%wide.region_6.7_spmd, body=%wide.region_5.6_spmd.sunk | while | flops 262149 | bytes 3670343 | solution.py:434
  312.2 2.4 bitcast_add_fusion.5
  316.1 2.4 bitcast_add_fusion.5
  319.9 2.4 bitcast_add_fusion.5
  323.7 2.4 bitcast_add_fusion.5
  327.6 2.4 bitcast_add_fusion.5
  331.5 2.4 bitcast_add_fusion.5
  335.4 2.4 bitcast_add_fusion.5
  339.3 2.4 bitcast_add_fusion.5
  343.2 2.4 bitcast_add_fusion.5
  347.1 2.4 bitcast_add_fusion.5
  351.0 2.4 bitcast_add_fusion.5
  354.9 2.4 bitcast_add_fusion.5
  358.8 2.4 bitcast_add_fusion.5
  362.7 2.4 bitcast_add_fusion.5
  366.6 2.4 bitcast_add_fusion.5
  370.5 2.4 bitcast_add_fusion.5
  374.4 2.4 bitcast_add_fusion.5
  378.3 2.4 bitcast_add_fusion.5
  382.2 2.4 bitcast_add_fusion.5
  386.0 2.4 bitcast_add_fusion.5
  389.9 2.4 bitcast_add_fusion.5
  393.7 2.4 bitcast_add_fusion.5
  397.6 2.5 bitcast_add_fusion.5
  401.5 2.4 bitcast_add_fusion.5
  405.4 2.4 bitcast_add_fusion.5
  409.2 2.4 bitcast_add_fusion.5
  413.1 2.4 bitcast_add_fusion.5
  417.0 2.4 bitcast_add_fusion.5
  420.8 2.4 bitcast_add_fusion.5
  424.7 2.4 bitcast_add_fusion.5
  428.5 2.4 bitcast_add_fusion.5
  432.4 2.4 bitcast_add_fusion.5
  436.3 2.4 bitcast_add_fusion.5
  440.1 2.4 bitcast_add_fusion.5
  443.9 2.4 bitcast_add_fusion.5
  447.8 2.4 bitcast_add_fusion.5
  451.6 2.4 bitcast_add_fusion.5
  455.5 2.4 bitcast_add_fusion.5
  459.3 2.4 bitcast_add_fusion.5
  463.2 2.4 bitcast_add_fusion.5
  467.0 2.4 bitcast_add_fusion.5
  470.9 2.4 bitcast_add_fusion.5
  474.7 2.4 bitcast_add_fusion.5
  478.5 2.4 bitcast_add_fusion.5
  482.4 2.4 bitcast_add_fusion.5
  486.2 2.4 bitcast_add_fusion.5
  490.0 2.4 bitcast_add_fusion.5
  493.9 2.4 bitcast_add_fusion.5
  497.7 2.4 bitcast_add_fusion.5
  501.5 2.4 bitcast_add_fusion.5
  505.4 2.4 bitcast_add_fusion.5
  509.2 2.4 bitcast_add_fusion.5
  513.0 2.4 bitcast_add_fusion.5
  516.9 2.4 bitcast_add_fusion.5
  520.7 2.4 bitcast_add_fusion.5
  524.5 2.4 bitcast_add_fusion.5
  553.8 3.2 fusion.3
  (253 shorter events, 131.0 us)
Async XLA Ops:
  7.2 122.6 %copy-start = (bf16[128,5120]{1,0:T(8,128)(2,1)S(1)}, bf16[128,5120]{1,0:T(8,128)(2,1)}, u32[]{:S(2)}) copy-start(bf16[128,5120]{1,0:T(8,128)(2,1)} %param.18) | copy-start | bytes 3932164
  7.2 194.4 %all-gather.6.cloned.1.call-start = ((), (), s32[]{:S(2)}) async-start(), calls=%async_computation.1 | async-start | bytes 34078720 | tf_op jit(solution)/shard_map/all_gather | solution.py:425
  10.1 187.9 %copy-start.2 = (bf16[128,1024]{0,1:T(8,128)(2,1)}, bf16[128,1024]{0,1:T(8,128)(2,1)S(1)}, u32[]{:S(2)}) copy-start(bf16[128,1024]{0,1:T(8,128)(2,1)S(1)} %copy.78) | copy-start | bytes 786436
  11.8 297.7 %all-gather.8.cloned.1.call-start = ((), (), s32[]{:S(2)}) async-start(), calls=%async_computation.2 | async-start | bytes 34078720 | tf_op jit(solution)/shard_map/all_gather | solution.py:425
  13.1 183.9 %copy-start.4 = (bf16[128,1024]{0,1:T(8,128)(2,1)}, bf16[128,1024]{0,1:T(8,128)(2,1)S(1)}, u32[]{:S(2)}) copy-start(bf16[128,1024]{0,1:T(8,128)(2,1)S(1)} %copy.83) | copy-start | bytes 786436
  15.5 544.6 %reduce-scatter.4.cloned.1.call-start = ((), (), s32[]{:S(2)}) async-start(), calls=%async_computation.3 | async-start | bytes 13312000
  197.5 4.1 copy-start.3
  201.7 3.2 copy-start.5
  310.7 252.2 %copy-start.1 = (bf16[128,5120]{1,0:T(8,128)(2,1)S(1)}, bf16[128,5120]{1,0:T(8,128)(2,1)}, u32[]{:S(2)}) copy-start(bf16[128,5120]{1,0:T(8,128)(2,1)} %param.18) | copy-start | bytes 3932164
  310.7 251.0 %copy-start.7 = (bf16[128,128]{1,0:T(8,128)(2,1)S(1)}, bf16[128,128]{1,0:T(8,128)(2,1)}, u32[]{:S(2)}) copy-start(bf16[128,128]{1,0:T(8,128)(2,1)} %get-tuple-element.360) | copy-start | bytes 98308
  310.7 251.6 %copy-start.6 = (bf16[128,128]{1,0:T(8,128)(2,1)S(1)}, bf16[128,128]{1,0:T(8,128)(2,1)}, u32[]{:S(2)}) copy-start(bf16[128,128]{1,0:T(8,128)(2,1)} %get-tuple-element.361) | copy-start | bytes 98308
Sparse Core Ops, SparseCore 0:
  12.0 156.1 all-gather.5
  171.0 138.5 all-gather.7
  314.5 155.4 reduce-scatter.3

commit v2 on v0

v2 whole, which is shorter than its diff:
```python
import functools
import jax
import jax.numpy as jnp
from jax import lax
from jax.experimental import pallas as pl
from jax.experimental.pallas import tpu as pltpu
from jax.sharding import PartitionSpec as P

HD = 128
NS = 128
HALF = 512
COLS = 1280
GROUPS = 5
ROWS = 128 * GROUPS
TK = 512
SCALE = HD ** (-0.5)
LOG2E = 1.4426950408889634
MESH = pl.DeviceIdType.MESH
F32 = jnp.float32
BF16 = jnp.bfloat16


def dot(a, b, ca, cb):
    return lax.dot_general(a, b, (((ca,), (cb,)), ((), ())), preferred_element_type=F32)


class Place:
    def __init__(self):
        self.me = lax.axis_index("ctx")
        self.y = lax.axis_index("fsdp")
        self.core = self.me % 2
        self.z = (self.me // 2) % 8
        self.x = self.me // 16

    def dev(self, x, z, core):
        return ((x * 8 + z) * 2 + core, self.y)

    def across(self, step):
        return (self.me, (self.y + step) % 4)


def exact(a, b):
    return lax.dot_general(
        a, b, (((1,), (0,)), ((), ())), preferred_element_type=F32, precision=lax.Precision.HIGHEST
    )


def add16(a, b):
    return (a.astype(F32) + b.astype(F32)).astype(BF16)


def in_turns(order, *steps):
    for i in order:
        next(steps[i], None)
    for step in steps:
        for _ in step:
            pass


def kernel(q_ref, k_ref, v_ref, do_ref, lg_ref, f_ref, w_ref, r_ref, ld_ref, g_ref,
           dq_ref, dk_ref, dv_ref, pg_ref, feed_ref, write_ref, read_ref,
           kv, dkv, pst, qs, dot_ref, mst, l_ref, top_ref, acc, sib,
           x1, x2, z1, xin, zin,
           mo4, lg4, pj, psib, pz,
           lds, a_ref, at_ref, tx, fw, gh, fed, inner,
           mine_s, sx, sy, lt, ls, t16, cdl, in1, xt, out2, in2, vx, vy, si, gn,
           ag_send, ag_recv, sib_recv, rs_send, rs_sib_send, rs_sib, rs_x, rs_z, rs_xin, rs_zin,
           mo_send, mo_recv, lg_send, lg_recv, lg_own, lg_y, pj_send, pj_sib, pj_z,
           s_pair, s_z, s_x, s_back, s_last):
    p = Place()
    me, x, z, core = p.me, p.x, p.z, p.core
    other = 1 - core

    barrier = pltpu.get_barrier_semaphore()

    def zz(s):
        return (z + s + 8) % 8

    xr, xl, xo = (x + 1) % 4, (x + 3) % 4, (x + 2) % 4
    partners = [p.dev(x, z, other)] + [p.dev(t, z, core) for t in (xr, xl, xo)]
    partners += [p.dev(x, zz(i), core) for i in range(1, 8)]
    partners += [p.across(1), p.across(3)]
    for t in partners:
        pl.semaphore_signal(barrier, inc=1, device_id=t, device_id_type=MESH)
    kv[core, x, z, 0] = k_ref[...]
    kv[core, x, z, 1] = v_ref[...]
    pl.semaphore_wait(barrier, 13)

    def push(c, bx, bz, half, target):
        if half is None:
            src, sem = kv.at[c, bx, bz], ag_recv.at[bx, bz, 0]
        else:
            src, sem = kv.at[c, bx, bz, half], ag_recv.at[bx, bz, half]
        pltpu.make_async_remote_copy(
            src_ref=src, dst_ref=src, send_sem=ag_send, recv_sem=sem,
            device_id=target, device_id_type=MESH).start()

    def sibling(c, bx, bz):
        pltpu.make_async_remote_copy(
            src_ref=kv.at[c, bx, bz], dst_ref=kv.at[c, bx, bz], send_sem=ag_send,
            recv_sem=sib_recv.at[bx, bz], device_id=p.dev(x, z, 1 - c), device_id_type=MESH).start()

    def got(c, bx, bz, half=None):
        if half is None:
            ref, sem = kv.at[c, bx, bz], ag_recv.at[bx, bz, 0]
        else:
            ref, sem = kv.at[c, bx, bz, half], ag_recv.at[bx, bz, half]
        pltpu.make_async_remote_copy(
            src_ref=ref, dst_ref=ref, send_sem=ag_send, recv_sem=sem,
            device_id=p.dev(x, z, 1 - c), device_id_type=MESH).wait_recv()

    @pl.when(core == 0)
    def _():
        push(0, x, z, None, p.dev(x, zz(1), 0))
        push(0, x, z, None, p.dev(x, zz(-1), 0))
        push(0, x, z, None, p.dev(xr, z, 0))
        push(0, x, z, None, p.dev(xl, z, 0))
        sibling(0, x, z)

    @pl.when(core == 1)
    def _():
        push(1, x, z, None, p.dev(xr, z, 1))
        push(1, x, z, None, p.dev(xl, z, 1))
        push(1, x, z, None, p.dev(x, zz(1), 1))
        push(1, x, z, None, p.dev(x, zz(-1), 1))
        sibling(1, x, z)

    for g in range(GROUPS):
        cols = pl.ds(g * 128, 128)
        qs[g * 128:(g + 1) * 128, :] = q_ref[:, cols]
        dot_ref[:, cols] = do_ref[:, cols].astype(F32).T

    def zero(i, c):
        dkv[i // 32, (i // 8) % 4, i % 8] = jnp.zeros((2, 128, 128), BF16)
        return c

    lax.fori_loop(0, 64, zero, 0)
    acc[...] = jnp.zeros_like(acc)
    l_ref[...] = jnp.zeros_like(l_ref)
    top_ref[...] = jnp.full_like(top_ref, -1e30)

    def pair_copy(src, dst, i):
        return pltpu.make_async_remote_copy(
            src_ref=src, dst_ref=dst, send_sem=s_pair.at[i, 0], recv_sem=s_pair.at[i, 1],
            device_id=p.dev(x, z, other), device_id_type=MESH)

    def states_alone():
        row = lax.broadcasted_iota(jnp.int32, (128, 128), 0)
        col = lax.broadcasted_iota(jnp.int32, (128, 128), 1)
        lds[...] = jnp.zeros_like(lds)
        lds[0:16, :] = ld_ref[...]
        running = exact((row >= col).astype(F32), lds[...].T)
        a_ref[...] = running
        at_ref[...] = running.T
        total = running[127:128, :]
        spread_heads = (
            lax.broadcasted_iota(jnp.int32, (128, 1024), 1) // 64
            == lax.broadcasted_iota(jnp.int32, (128, 1024), 0)
        ).astype(F32)
        tx[...] = exact(jnp.exp(total - running), spread_heads)
        fw[...] = (f_ref[...].astype(F32) * tx[...]).astype(BF16)
        gh[...] = (g_ref[...].astype(F32) * exact(jnp.exp(running), spread_heads)).astype(BF16)
        lt[...] = exact(jnp.broadcast_to(total, (8, 128)), spread_heads)
        for g in range(2):
            wide = slice(g * HALF, (g + 1) * HALF)
            narrow = slice(g * NS, (g + 1) * NS)
            state = dot(w_ref[:, narrow], fw[:, wide], 0, 0)
            back = dot(r_ref[:, narrow], gh[:, wide], 0, 0)

            @pl.when(core == 0)
            def _():
                mine_s[:, wide] = state
                sx[:, wide] = back.astype(BF16)

            @pl.when(core == 1)
            def _():
                mine_s[:, wide] = back
                sx[:, wide] = state.astype(BF16)

        pair_copy(sx, sy, 0).start()
        pair_copy(lt, ls, 1).start()
        yield
        low_half = col < 64

        def two(value):
            full = value.astype(F32)
            return jnp.concatenate(
                [jnp.where(low_half, full, 0.0), jnp.where(low_half, 0.0, full)], axis=0
            ).astype(BF16)

        for g in range(2):
            narrow = slice(g * NS, (g + 1) * NS)
            pairing = dot(w_ref[:, narrow], r_ref[:, narrow], 1, 1)
            inner[...] = jnp.zeros_like(inner)
            for k in range(4):
                lanes = slice(g * HALF + k * 128, g * HALF + (k + 1) * 128)
                head = g * 8 + 2 * k
                decays = []
                for h in (head, head + 1):
                    gap = at_ref[h:h + 1, :] - a_ref[:, h:h + 1]
                    decays.append(jnp.where(col >= row, jnp.exp(jnp.where(col >= row, gap, 0.0)), 0.0))
                grads = g_ref[:, lanes]
                cross = dot(two(f_ref[:, lanes]), grads, 1, 1)
                inner[...] += decays[0] * cross[0:128] + decays[1] * cross[128:256]
                mixed = jnp.concatenate([d * pairing for d in decays], axis=1).astype(BF16)
                fed[:, lanes] = dot(mixed, two(grads), 1, 0)
                yield
            inner16 = inner[...].astype(BF16)
            write_ref[:, narrow] = dot(inner16, r_ref[:, narrow], 1, 0)
            read_ref[:, narrow] = dot(inner16, w_ref[:, narrow], 0, 0)

    right, left = p.dev(x, zz(1), core), p.dev(x, zz(-1), core)
    xright, xleft = p.dev(xr, z, core), p.dev(xl, z, core)

    def spread_x(bz):
        push(0, x, bz, None, xright)
        push(0, x, bz, None, xleft)
        sibling(0, x, bz)

    def across(bz):
        got(0, xl, bz)
        push(0, xl, bz, 0, xright)
        sibling(0, xl, bz)
        got(0, xr, bz)
        push(0, xr, bz, 1, xleft)
        sibling(0, xr, bz)

    def opposite(bz):
        got(0, xo, bz, 0)
        got(0, xo, bz, 1)
        sibling(0, xo, bz)

    def row_step(s):
        got(0, x, zz(-s))
        push(0, x, zz(-s), None if s < 3 else 0, right)
        spread_x(zz(-s))
        got(0, x, zz(s))
        push(0, x, zz(s), None if s < 3 else 1, left)
        spread_x(zz(s))

    def spread_z(bx):
        push(1, bx, z, None, right)
        push(1, bx, z, None, left)
        sibling(1, bx, z)

    def along(bx, s):
        got(1, bx, zz(-s))
        push(1, bx, zz(-s), None if s < 3 else 0, right)
        sibling(1, bx, zz(-s))
        got(1, bx, zz(s))
        push(1, bx, zz(s), None if s < 3 else 1, left)
        sibling(1, bx, zz(s))

    def first(k):
        if k == 0:
            row_step(1)
        elif k == 1:
            across(z)
            row_step(2)
        elif k == 2:
            across(zz(-1))
            across(zz(1))
            opposite(z)
            row_step(3)
        elif k == 3:
            opposite(zz(-1))
            opposite(zz(1))
            across(zz(-2))
            across(zz(2))
            got(0, x, zz(4), 0)
            got(0, x, zz(4), 1)
            spread_x(zz(4))
        elif k == 4:
            across(zz(-3))
            across(zz(3))
            opposite(zz(-2))
            opposite(zz(2))
        elif k == 5:
            across(zz(4))
            opposite(zz(-3))
            opposite(zz(3))
        else:
            opposite(zz(4))

    def second(k):
        if k == 0:
            got(1, xl, z)
            push(1, xl, z, 0, xright)
            spread_z(xl)
            got(1, xr, z)
            push(1, xr, z, 1, xleft)
            spread_z(xr)
            along(x, 1)
        elif k == 1:
            got(1, xo, z, 0)
            got(1, xo, z, 1)
            spread_z(xo)
            along(xl, 1)
            along(xr, 1)
        elif k == 2:
            along(x, 2)
            along(xo, 1)
        elif k == 3:
            along(xl, 2)
            along(xr, 2)
            along(x, 3)
            along(xo, 2)
        elif k == 4:
            along(xl, 3)
            along(xr, 3)
            along(xo, 3)
        elif k == 5:
            for bx in (x, xl):
                got(1, bx, zz(4), 0)
                got(1, bx, zz(4), 1)
                sibling(1, bx, zz(4))
        else:
            for bx in (xr, xo):
                got(1, bx, zz(4), 0)
                got(1, bx, zz(4), 1)
                sibling(1, bx, zz(4))

    def gather(k):
        @pl.when(core == 0)
        def _():
            first(k)

        @pl.when(core == 1)
        def _():
            second(k)

    def order(k, n):
        return k + core * (n - 1 - 2 * k)

    def z_copy(i, src, dst, sems, slot):
        t = zz(i)
        return pltpu.make_async_remote_copy(
            src_ref=src.at[slot(t)], dst_ref=dst.at[z], send_sem=sems.at[0, i], recv_sem=sems.at[1, z],
            device_id=p.dev(x, t, core), device_id_type=MESH)

    def z_wait(i, src, dst, sems, slot):
        t = zz(i)
        pltpu.make_async_remote_copy(
            src_ref=src.at[slot(t)], dst_ref=dst.at[t], send_sem=sems.at[0, i], recv_sem=sems.at[1, t],
            device_id=p.dev(x, t, core), device_id_type=MESH).wait()

    def at_target(t):
        return t

    def at_home(t):
        return z

    def states_join():
        pair_copy(sx, sy, 0).wait()
        pair_copy(lt, ls, 1).wait()
        joined = jnp.exp(ls[0:1, :]) * mine_s[...] + sy[...].astype(F32)
        t16[...] = joined.astype(BF16).reshape(8, 16, 1024)
        cdl[z] = lt[...] + ls[...]
        for i in range(1, 8):
            z_copy(i, t16, in1, s_z.at[0], at_target).start()
            z_copy(i, cdl, cdl, s_z.at[1], at_home).start()
        in1[z] = t16[z]

    def x_copy(i, t):
        return pltpu.make_async_remote_copy(
            src_ref=xt.at[i], dst_ref=xt.at[i], send_sem=s_x.at[0, (t - x + 4) % 4], recv_sem=s_x.at[1, i],
            device_id=p.dev(t, z, core), device_id_type=MESH)

    def along_row(state, keep):
        for k in range(8):
            c = order(k, 8)
            if keep:
                out2[c] = state.astype(BF16)
            state = jnp.exp(cdl[c, 0:1, :]) * state + in1[c].astype(F32)
        return state

    def states_row():
        for i in range(1, 8):
            z_wait(i, t16, in1, s_z.at[0], at_target)
            z_wait(i, cdl, cdl, s_z.at[1], at_home)
        xt[x, 0:16, :] = along_row(jnp.zeros((16, 1024), F32), False)
        summed = cdl[0]
        for k in range(1, 8):
            summed = summed + cdl[k]
        xt[x, 16:24, :] = summed
        for t in (xr, xl, xo):
            x_copy(x, t).start()

    def states_back():
        for t in (xr, xl, xo):
            x_copy(x, t).wait_send()
            x_copy(t, t).wait_recv()
        state = jnp.zeros((16, 1024), F32)
        mine_at = order(0, 4) + x - 2 * core * x
        for k in range(3):
            c = order(k, 4)
            later = jnp.exp(xt[c, 16:17, :]) * state + xt[c, 0:16, :]
            state = jnp.where(k < mine_at, later, state)
        along_row(state, True)
        for i in range(1, 8):
            z_copy(i, out2, in2, s_back, at_target).start()
        in2[z] = out2[z]

    def states_last():
        for i in range(1, 8):
            z_wait(i, out2, in2, s_back, at_target)
        entered = in2[...].reshape(128, 1024)
        vx[...] = (jnp.exp(lt[0:1, :]) * entered.astype(F32) + mine_s[...]).astype(BF16)
        pair_copy(vx, vy, 2).start()

    def columns(i):
        return pl.ds(pl.multiple_of(i * COLS, 128), COLS)

    def quarter(y):
        return pl.ds(pl.multiple_of(((y + 4) % 4) * 32, 32), 32)

    def lg_copy(i, t):
        return pltpu.make_async_remote_copy(
            src_ref=lg_ref.at[quarter(p.y), columns(t)], dst_ref=lg4.at[i, quarter(p.y)],
            send_sem=lg_send, recv_sem=lg_recv.at[i],
            device_id=p.dev(t, z, core), device_id_type=MESH)

    def lg_turn(step):
        ref = lg4.at[:, quarter(p.y)]
        return pltpu.make_async_remote_copy(
            src_ref=ref, dst_ref=ref, send_sem=lg_y.at[0, step // 2], recv_sem=lg_y.at[1, step // 2],
            device_id=p.across(step), device_id_type=MESH)

    def lg_from(step):
        ref = lg4.at[:, quarter(p.y + step)]
        return pltpu.make_async_remote_copy(
            src_ref=ref, dst_ref=ref, send_sem=lg_y.at[0, 0], recv_sem=lg_y.at[1, 1 - step // 2],
            device_id=p.across(step), device_id_type=MESH)

    def lg_pass(step, y):
        ref = lg4.at[pl.ds(step - 1, 2), quarter(y)]
        return pltpu.make_async_remote_copy(
            src_ref=ref, dst_ref=ref, send_sem=lg_y.at[0, 2 + step // 2], recv_sem=lg_y.at[1, 2 + step // 2],
            device_id=p.across(step), device_id_type=MESH)

    def mo_copy(i, t):
        return pltpu.make_async_remote_copy(
            src_ref=mo4.at[i], dst_ref=mo4.at[i], send_sem=mo_send, recv_sem=mo_recv.at[i],
            device_id=p.dev(t, z, core), device_id_type=MESH)

    lg_mine = pltpu.make_async_copy(
        lg_ref.at[quarter(p.y), columns(x)], lg4.at[x, quarter(p.y)], lg_own)
    lg_mine.start()
    for t in (xr, xl, xo):
        lg_copy(x, t).start()

    diag = me // 4
    zp = z // 2

    def keys(j, which):
        return kv[:, j // 4, pl.ds(2 * (j % 4), 2), which].reshape(TK, HD)

    def forward(j, masked):
        top = top_ref[...]
        s = dot(keys(j, 0), qs[...], 1, 1)
        if masked:
            r = lax.broadcasted_iota(jnp.int32, (TK, ROWS), 0)
            c = lax.broadcasted_iota(jnp.int32, (TK, ROWS), 1)
            pos = ((j * 4 + ((r // 128) % 2) * 2 + r // 256) * 128) + r % 128
            s = jnp.where(pos <= me * 128 + c % 128, s, -1e30)
        new = jnp.maximum(top, jnp.max(s, axis=0, keepdims=True))
        w = jnp.exp2((s - new) * (SCALE * LOG2E))
        shrink = jnp.exp2((top - new) * (SCALE * LOG2E))
        l_ref[...] = l_ref[...] * shrink + jnp.sum(w, axis=0, keepdims=True)
        w16 = w.astype(BF16)
        pst[j] = w16
        mst[j] = new
        top_ref[...] = new
        acc[...] = acc[...] * shrink + dot(keys(j, 1), w16, 0, 0)

    def sib_wait(bx, bz):
        pltpu.make_async_remote_copy(
            src_ref=kv.at[other, bx, bz], dst_ref=kv.at[other, bx, bz], send_sem=ag_send,
            recv_sem=sib_recv.at[bx, bz], device_id=p.dev(x, z, other), device_id_type=MESH).wait_recv()

    def column_ready(i):
        c = (zp + i) % 4

        def one(b, carry):
            sib_wait(b // 2, 2 * c + b % 2)
            return carry

        lax.fori_loop(0, 8, one, 0)

    def column(i, start, stop):
        c = (zp + i) % 4

        def one(b, carry):
            forward(4 * b + c, False)
            return carry

        lax.fori_loop(start, jnp.minimum(stop, (diag - c + 3) // 4), one, 0)

    alone = states_alone()
    next(alone)
    gather(0)
    next(alone)
    next(alone)
    gather(1)
    next(alone)
    next(alone)
    gather(2)
    next(alone)
    next(alone)
    gather(3)
    for _ in alone:
        pass
    lg_mine.wait()
    for t in (xr, xl, xo):
        lg_copy(t, t).wait_recv()
    lg_turn(1).start()
    lg_turn(3).start()
    column_ready(0)
    forward(diag, True)
    gather(4)
    column(0, 0, 4)
    states_join()
    gather(5)
    column_ready(1)
    column_ready(3)
    column(1, 0, 4)
    gather(6)
    for step in (1, 3):
        lg_from(step).wait_recv()
    lg_pass(1, p.y - 1).start()
    lg_pass(3, p.y + 1).start()
    column(3, 0, 4)
    column_ready(2)
    column(2, 0, 4)
    for ref in (kv.at[0], kv.at[1, pl.ds(0, 3)], kv.at[1, 3, pl.ds(0, 7)]):
        pltpu.make_async_copy(ref, ref, ag_send).wait()
    top = top_ref[...]
    inv = 1.0 / l_ref[...]
    out_t = acc[...] * inv
    delta = jnp.sum(out_t * dot_ref[...], axis=0, keepdims=True)
    for g in range(GROUPS):
        mo4[x, :, g * 128:(g + 1) * 128] = out_t[:, g * 128:(g + 1) * 128].T.astype(BF16)
    for t in (xr, xl, xo):
        mo_copy(x, t).start()
    states_row()
    acc[...] = jnp.zeros_like(acc)

    def sib_copy(j):
        pair = pl.ds(2 * (j % 4), 2)
        return pltpu.make_async_remote_copy(
            src_ref=dkv.at[other, j // 4, pair], dst_ref=sib.at[j // 4, pair],
            send_sem=rs_sib_send.at[j], recv_sem=rs_sib.at[j],
            device_id=p.dev(x, z, other), device_id_type=MESH)

    def sib_add(j):
        pair = pl.ds(2 * (j % 4), 2)
        sib_copy(j).wait()
        dkv[core, j // 4, pair] = add16(dkv[core, j // 4, pair], sib[j // 4, pair])

    def backward(j, c):
        factor = jnp.exp2((mst[j] - top) * (SCALE * LOG2E)) * inv
        grad = (dot_ref[...] * factor).astype(BF16)
        dw = dot(keys(j, 1), grad, 1, 0)
        w16 = pst[j]
        ds = (w16.astype(F32) * (dw - delta * factor)).astype(BF16)
        dk = dot(ds, qs[...], 1, 0) * SCALE
        dv = dot(w16, grad, 1, 1)
        acc[...] = acc[...] + dot(keys(j, 0), ds, 0, 0)
        dkv[:, j // 4, pl.ds(2 * (j % 4), 2), 0] = dk.astype(BF16).reshape(2, 2, 128, 128)
        dkv[:, j // 4, pl.ds(2 * (j % 4), 2), 1] = dv.astype(BF16).reshape(2, 2, 128, 128)
        sib_copy(j).start()
        return c

    def place(i):
        return (2 - i - i * (i - 1) // 2 + 8) % 4

    def shell(k, work):
        n = 4 - k

        def one(t, c):
            straight = t < n
            row = jnp.where(straight, k, k + 1 + t - n)
            column = jnp.where(straight, k + t, k)
            j = 4 * ((x + place(row)) % 4) + (zp + place(column)) % 4

            @pl.when(j <= diag)
            def _():
                work(j)

            return c

        lax.fori_loop(0, 2 * n - 1, one, 0)

    def backward_shell(k):
        shell(k, lambda j: backward(j, 0))

    def finish_shell(k):
        shell(k, sib_add)

    def remote(src, dst, sem, target, send=rs_send):
        return pltpu.make_async_remote_copy(
            src_ref=src, dst_ref=dst, send_sem=send, recv_sem=sem,
            device_id=target, device_id_type=MESH)

    def z_ring(mine, inbox, sems, send):
        right, left = p.dev(x, zz(1), core), p.dev(x, zz(-1), core)
        ra = remote(mine(zz(4), 0), inbox(0, 0, 0), sems.at[0, 0], right, send)
        la = remote(mine(zz(4), 1), inbox(1, 0, 1), sems.at[0, 1], left, send)
        ra.start()
        la.start()
        yield
        for s in (1, 2, 3):
            d = 4 - s
            h = 0 if s == 1 else None
            ra.wait_recv()
            ref = mine(zz(d), h)
            ref[...] = add16(ref[...], inbox(0, s - 1, h)[...])
            ra = remote(mine(zz(d)), inbox(0, s), sems.at[s, 0], right, send)
            ra.start()
            h = 1 if s == 1 else None
            la.wait_recv()
            ref = mine(zz(-d), h)
            ref[...] = add16(ref[...], inbox(1, s - 1, h)[...])
            la = remote(mine(zz(-d)), inbox(1, s), sems.at[s, 1], left, send)
            la.start()
            yield
        ra.wait_recv()
        la.wait_recv()

    def projection():
        for t in (xr, xl, xo):
            mo_copy(t, t).wait_recv()
        lg_pass(1, p.y + 2).wait_recv()
        lg_pass(3, p.y + 2).wait_recv()
        lg_turn(1).wait_send()
        lg_turn(3).wait_send()
        lg_pass(1, p.y - 1).wait_send()
        lg_pass(3, p.y + 1).wait_send()
        sent = lg4.at[pl.ds(0, 3), pl.ds(0, 32)]
        pltpu.make_async_copy(sent, sent, lg_send).wait()
        pltpu.make_async_copy(mo4.at[pl.ds(0, 3)], mo4.at[pl.ds(0, 3)], mo_send).wait()
        outs = mo4[...].reshape(512, ROWS)
        for i in range(2):
            part = dot(lg4[:, :, i * 640:(i + 1) * 640].reshape(512, 640), outs, 0, 0)
            for k in range(8):
                pj[k % 2, i * 4 + k // 2] = part[k * 80:(k + 1) * 80].astype(BF16)
        swap = remote(pj.at[other], psib, pj_sib, p.dev(x, z, other), pj_send)
        swap.start()
        yield
        swap.wait_recv()

        def one(b, c):
            pj[core, b] = add16(pj[core, b], psib[b])
            return c

        lax.fori_loop(0, 8, one, 0)

        def half_of(ref, h):
            return ref if h is None else ref.at[pl.ds(0, 48)] if h == 0 else ref.at[pl.ds(48, 32)]

        yield from z_ring(
            lambda i, h=None: half_of(pj.at[core, i], h),
            lambda way, s, h=None: half_of(pz.at[way, s], h), pj_z, pj_send)
        pg_ref[...] = pj[core, z].astype(F32) + pz[0, 3].astype(F32) + pz[1, 3].astype(F32)

    proj = projection()

    def x_half(way):
        t, target = (xo, xright) if way == 0 else (xo, xleft)
        return remote(dkv.at[0, t, :, way], x1.at[way], rs_x.at[0, way], target)

    def x_full(way):
        t, target = (xr, xright) if way == 0 else (xl, xleft)
        return remote(dkv.at[0, t], x2.at[way], rs_x.at[1, way], target)

    def z_half(way):
        return remote(dkv.at[1, :, zz(4), way], z1.at[way, 0, :, way], rs_z.at[0, way], right if way == 0 else left)

    def z_full(way, s):
        t, target = (zz(4 - s), right) if way == 0 else (zz(s - 4), left)
        return remote(dkv.at[1, :, t], z1.at[way, s], rs_z.at[s, way], target)

    def x_next(way):
        x_half(way).wait_recv()
        t = xr if way == 0 else xl
        dkv[0, t, :, way] = add16(dkv[0, t, :, way], x1[way])
        x_full(way).start()

    def z_next(way, s):
        t = zz(4 - s) if way == 0 else zz(s - 4)
        if s == 1:
            z_half(way).wait_recv()
            dkv[1, :, t, way] = add16(dkv[1, :, t, way], z1[way, 0, :, way])
        else:
            z_full(way, s - 1).wait_recv()
            dkv[1, :, t] = add16(dkv[1, :, t], z1[way, s - 1])
        z_full(way, s).start()

    def by_core(zero, one):
        pl.when(core == 0)(zero)
        pl.when(core == 1)(one)

    def both(f):
        f(0)
        f(1)

    backward_shell(0)
    finish_shell(0)
    by_core(lambda: both(lambda w: x_half(w).start()), lambda: both(lambda w: z_half(w).start()))
    states_back()
    backward_shell(1)
    next(proj, None)
    finish_shell(1)
    by_core(lambda: x_next(0), lambda: z_next(0, 1))
    backward_shell(2)
    next(proj, None)
    finish_shell(2)

    def third():
        z_next(1, 1)
        z_next(0, 2)

    by_core(lambda: x_next(1), third)
    backward_shell(3)
    states_last()
    finish_shell(3)
    for g in range(GROUPS):
        dq_ref[:, g * 128:(g + 1) * 128] = (acc[:, g * 128:(g + 1) * 128] * SCALE).T.astype(BF16)

    def sum3(a, b, c):
        return (a.astype(F32) + b.astype(F32) + c.astype(F32)).astype(BF16)

    def x_sum():
        both(lambda w: x_full(w).wait_recv())

        def one(b, c):
            dkv[0, x, b] = sum3(dkv[0, x, b], x2[0, b], x2[1, b])
            return c

        lax.fori_loop(0, 8, one, 0)
        for i in range(1, 8):
            z_in(i).start()

    def z_in(i):
        t = zz(i)
        return remote(dkv.at[0, x, t], zin.at[z], rs_zin.at[z], p.dev(x, t, 0))

    def z_sum():
        both(lambda w: z_full(w, 3).wait_recv())

        def one(b, c):
            dkv[1, b, z] = sum3(dkv[1, b, z], z1[0, 3, b], z1[1, 3, b])
            return c

        lax.fori_loop(0, 4, one, 0)
        for i in range(1, 4):
            x_in(i).start()

    def x_in(i):
        t = (x + i) % 4
        return remote(dkv.at[1, t, z], xin.at[x], rs_xin.at[x], p.dev(t, z, 1))

    def keys_out(parts):
        for ref, h in ((dk_ref, 0), (dv_ref, 1)):
            total = parts[0][h].astype(F32)
            for part in parts[1:]:
                total = total + part[h].astype(F32)
            ref[...] = total.astype(BF16)

    def last_zero():
        for i in range(1, 8):
            t = zz(i)
            remote(dkv.at[0, x, t], zin.at[t], rs_zin.at[t], p.dev(x, t, 0)).wait_recv()
        keys_out([dkv.at[0, x, z]] + [zin.at[zz(i)] for i in range(1, 8)])

    def last_one():
        for i in range(1, 4):
            t = (x + i) % 4
            remote(dkv.at[1, t, z], xin.at[t], rs_xin.at[t], p.dev(t, z, 1)).wait_recv()
        keys_out([dkv.at[1, x, z]] + [xin.at[(x + i) % 4] for i in range(1, 4)])

    def states():
        pair_copy(vx, vy, 2).wait()

        @pl.when(core == 0)
        def _():
            si[...] = in2[...].reshape(128, 1024)
            gn[...] = vy[...]

        @pl.when(core == 1)
        def _():
            gn[...] = in2[...].reshape(128, 1024)
            si[...] = vy[...]

        for g in range(2):
            narrow = slice(g * NS, (g + 1) * NS)
            wide = slice(g * HALF, (g + 1) * HALF)
            full = fed[:, wide] + tx[:, wide] * dot(w_ref[:, narrow], gn[:, wide], 1, 0)
            feed_ref[:, wide] = full.astype(BF16)
            yield
            write_ref[:, narrow] += dot(fw[:, wide], gn[:, wide], 1, 1)
            read_ref[:, narrow] += dot(gh[:, wide], si[:, wide], 1, 1)
            yield

    final = states()
    by_core(x_sum, lambda: z_next(1, 2))
    next(final)
    next(proj, None)
    by_core(lambda: None, lambda: z_next(0, 3))
    next(final)
    by_core(lambda: None, lambda: z_next(1, 3))
    next(proj, None)
    for _ in final:
        pass
    by_core(lambda: None, z_sum)
    next(proj, None)
    by_core(last_zero, last_one)
    for _ in proj:
        pass

    for ref in (kv.at[0, pl.ds(0, 3)], kv.at[0, 3, pl.ds(0, 7)]):
        pltpu.make_async_copy(ref, ref, rs_send).wait()
    for ref in (pj.at[0], pj.at[1, pl.ds(0, 7)]):
        pltpu.make_async_copy(ref, ref, pj_send).wait()


def copy_kernel(*refs):
    for i in range(7):
        refs[7 + i][...] = refs[i][...]


def per_device(query_rows, key_rows, value_rows, mixed_grad, layer_grad,
               state_feed, write_map, read_map, log_decay, scan_grad):
    vm = pl.BlockSpec(memory_space=pltpu.VMEM)
    dma = pltpu.SemaphoreType.DMA

    def out(shape, dtype):
        return jax.ShapeDtypeStruct(shape, dtype)

    shapes = (
            out((128, ROWS), BF16),
            out((128, 128), BF16),
            out((128, 128), BF16),
            out((80, ROWS), F32),
            out((128, 1024), BF16),
            out((128, 256), F32),
            out((128, 256), F32),
    )
    results = pl.pallas_call(
        kernel,
        out_shape=shapes,
        in_specs=[vm] * 4 + [pl.BlockSpec(memory_space=pl.ANY)] + [vm] * 5,
        out_specs=(vm,) * 7,
        scratch_shapes=[
            pltpu.VMEM((2, 4, 8, 2, 128, 128), BF16),
            pltpu.VMEM((2, 4, 8, 2, 128, 128), BF16),
            pltpu.VMEM((16, TK, ROWS), BF16),
            pltpu.VMEM((ROWS, HD), BF16),
            pltpu.VMEM((HD, ROWS), F32),
            pltpu.VMEM((16, 1, ROWS), F32),
            pltpu.VMEM((1, ROWS), F32),
            pltpu.VMEM((1, ROWS), F32),
            pltpu.VMEM((HD, ROWS), F32),
            pltpu.VMEM((4, 8, 2, 128, 128), BF16),
            pltpu.VMEM((2, 8, 128, 128), BF16),
            pltpu.VMEM((2, 8, 2, 128, 128), BF16),
            pltpu.VMEM((2, 4, 4, 2, 128, 128), BF16),
            pltpu.VMEM((4, 2, 128, 128), BF16),
            pltpu.VMEM((8, 2, 128, 128), BF16),
            pltpu.VMEM((4, 128, ROWS), BF16),
            pltpu.VMEM((4, 128, COLS), BF16),
            pltpu.VMEM((2, 8, 80, ROWS), BF16),
            pltpu.VMEM((8, 80, ROWS), BF16),
            pltpu.VMEM((2, 4, 80, ROWS), BF16),
            pltpu.VMEM((128, 128), F32),
            pltpu.VMEM((128, 128), F32),
            pltpu.VMEM((128, 128), F32),
            pltpu.VMEM((128, 1024), F32),
            pltpu.VMEM((128, 1024), BF16),
            pltpu.VMEM((128, 1024), BF16),
            pltpu.VMEM((128, 1024), F32),
            pltpu.VMEM((128, 128), F32),
            pltpu.VMEM((128, 1024), F32),
            pltpu.VMEM((128, 1024), BF16),
            pltpu.VMEM((128, 1024), BF16),
            pltpu.VMEM((8, 1024), F32),
            pltpu.VMEM((8, 1024), F32),
            pltpu.VMEM((8, 16, 1024), BF16),
            pltpu.VMEM((8, 8, 1024), F32),
            pltpu.VMEM((8, 16, 1024), BF16),
            pltpu.VMEM((4, 24, 1024), F32),
            pltpu.VMEM((8, 16, 1024), BF16),
            pltpu.VMEM((8, 16, 1024), BF16),
            pltpu.VMEM((128, 1024), BF16),
            pltpu.VMEM((128, 1024), BF16),
            pltpu.VMEM((128, 1024), BF16),
            pltpu.VMEM((128, 1024), BF16),
            dma, dma((4, 8, 2)), dma((4, 8)),
            dma, dma((16,)), dma((16,)), dma((2, 2)), dma((4, 2)), dma((4,)), dma((8,)),
            dma, dma((4,)), dma, dma((4,)), dma, dma((2, 4)), dma, dma, dma((4, 2)),
            dma((3, 2)), dma((2, 2, 8)), dma((2, 4)), dma((2, 8)), dma,
        ],
        compiler_params=pltpu.CompilerParams(
            collective_id=0, has_side_effects=True, vmem_limit_bytes=58 * 2**20
        ),
    )(query_rows, key_rows, value_rows, mixed_grad, layer_grad,
      state_feed, write_map, read_map, log_decay.T, scan_grad)
    return pl.pallas_call(
        copy_kernel,
        out_shape=shapes,
        in_specs=[vm] * 7,
        out_specs=(vm,) * 7,
    )(*results)


def solution(mesh):
    split = P("ctx", "fsdp")
    return jax.shard_map(
        per_device,
        mesh=mesh,
        in_specs=(split,) * 4 + (P("ctx", None),) + (split,) * 5,
        out_specs=(split,) * 7,
        check_vma=False,
    )
```

time: 923 us -> 98.4 us (0.11); the launches traced: 912 us -> 96.5 us
  waiting for transfers between devices: 562 us -> 0 us
  blocking collectives: 165 us -> 0 us
  local copies, waits for them, and re-layouts: 120 us -> 0 us
  Pallas kernels: 0 us -> 95.9 us
  matrix products: 29.4 us -> 0 us
  other arithmetic: 17.5 us -> 0 us
  between operations: 14.4 us -> 0.64 us
    all_gather x4 -> x0, waiting for transfers between devices: 334 us -> none  [the longest x2 177 us: entering(): gathered = jax.tree.map(lambda a: lax.all_gather(a, axis), part)]
    all_gather x1 -> x0, blocking collectives: 165 us -> none  [entering(): gathered = jax.tree.map(lambda a: lax.all_gather(a, axis), part)]
    unnamed x7 -> x0, waiting for transfers between devices: 155 us -> none
    pallas_call x0 -> x2, Pallas kernels: none -> 95.9 us  [the longest x1 93.7 us: per_device(): pl.pallas_call(kernel, out_shape=shapes, in_specs=[vm] * 4 + [pl.BlockSpe...]
    dynamic_slice x126 -> x0, local copies, waits for them, and re-layouts: 90.7 us -> none  [one(): lax.dynamic_index_in_dim(a, source, 0, False)]
    reduce_scatter x1 -> x0, waiting for transfers between devices: 73.5 us -> none  [per_device(): lax.psum_scatter(pair_acc, 'ctx', scatter_dimension=0, tiled=True)]
    dot_general x18 -> x0, matrix products: 29.4 us -> none  [the longest x1 6.63 us: per_device(): lax.dot_general(layer_grad, mixed_out, (((0,), (0,)), ((), ())), preferre...]
    unnamed x43 -> x0, local copies, waits for them, and re-layouts: 21.9 us -> none
  transfers between devices with their start and end apart: 6 -> 0, of which waited for: 6 -> 0; matrix products, arithmetic and copies ran while one was open for 17% -> 0% of each run, Pallas kernels for 0% -> 0%
where the time goes in v2:
time: 98.4 us; the launch traced here: 96.5 us
  Pallas kernels  95.9 us (97%)
    pallas_call x1, Pallas kernels, per_device(): pl.pallas_call(kernel, out_shape=shapes, in_specs=[vm] * 4 + [pl.BlockSpe...  93.7 us
    pallas_call x1, Pallas kernels, per_device(): pl.pallas_call(copy_kernel, out_shape=shapes, in_specs=[vm] * 7, out_spec...  2.2 us

profile of v2, /device:TPU:1, one launch (start us, length us, event | category | flops | bytes accessed | tf_op | source)
XLA Modules:
  0.0 96.5 jit_solution(2584304736852930450)
XLA Ops:
  0.6 93.7 %shard_map.153 = (bf16[128,640]{1,0:T(8,128)(2,1)}, bf16[128,128]{1,0:T(8,128)(2,1)}, bf16[128,128]{1,0:T(8,128)(2,1)}, f32[80,640]{1,0:T(8,128)}, bf16[128,1024...) custom-call(bf16[128,640]{1,0:T(8,128)(2,1)} %q_ref.1, bf16[128,128]{1,0:T(8,128)(2,1)} %k_ref.1, ...), custom_call_target="tpu_custom_call" | custom-call | tf_op jit(solution)/shard_map/pallas_call | solution.py:849
  94.3 2.2 %shard_map.154 = (bf16[128,640]{1,0:T(8,128)(2,1)}, bf16[128,128]{1,0:T(8,128)(2,1)}, bf16[128,128]{1,0:T(8,128)(2,1)}, f32[80,640]{1,0:T(8,128)}, bf16[128,1024...) custom-call(bf16[128,640]{1,0:T(8,128)(2,1)} %get-tuple-element.14.refs_0_, ...), custom_call_target="tpu_custom_call" | custom-call | tf_op jit(solution)/shard_map/pallas_call | solution.py:908

commit v3 on v2

--- a/solution.py
+++ b/solution.py
@@ -46,7 +46,7 @@
 
 
 def add16(a, b):
-    return (a.astype(F32) + b.astype(F32)).astype(BF16)
+    return a + b
 
 
 def in_turns(order, *steps):
@@ -121,6 +121,7 @@
     def _():
         push(1, x, z, None, p.dev(xr, z, 1))
         push(1, x, z, None, p.dev(xl, z, 1))
+        push(1, x, z, None, p.dev(xo, z, 1))
         push(1, x, z, None, p.dev(x, zz(1), 1))
         push(1, x, z, None, p.dev(x, zz(-1), 1))
         sibling(1, x, z)
@@ -285,16 +286,13 @@
     def second(k):
         if k == 0:
             got(1, xl, z)
-            push(1, xl, z, 0, xright)
             spread_z(xl)
             got(1, xr, z)
-            push(1, xr, z, 1, xleft)
             spread_z(xr)
             along(x, 1)
+            got(1, xo, z)
+            spread_z(xo)
         elif k == 1:
-            got(1, xo, z, 0)
-            got(1, xo, z, 1)
-            spread_z(xo)
             along(xl, 1)
             along(xr, 1)
         elif k == 2:
@@ -530,6 +528,7 @@
     lg_pass(1, p.y - 1).start()
     lg_pass(3, p.y + 1).start()
     column(3, 0, 4)
+    states_row()
     column_ready(2)
     column(2, 0, 4)
     for ref in (kv.at[0], kv.at[1, pl.ds(0, 3)], kv.at[1, 3, pl.ds(0, 7)]):
@@ -542,7 +541,6 @@
         mo4[x, :, g * 128:(g + 1) * 128] = out_t[:, g * 128:(g + 1) * 128].T.astype(BF16)
     for t in (xr, xl, xo):
         mo_copy(x, t).start()
-    states_row()
     acc[...] = jnp.zeros_like(acc)
 
     def sib_copy(j):
@@ -574,13 +572,9 @@
     def place(i):
         return (2 - i - i * (i - 1) // 2 + 8) % 4
 
-    def shell(k, work):
-        n = 4 - k
-
+    def shell(k, whole_column, work):
         def one(t, c):
-            straight = t < n
-            row = jnp.where(straight, k, k + 1 + t - n)
-            column = jnp.where(straight, k + t, k)
+            row, column = (t, k) if whole_column else (k, t)
             j = 4 * ((x + place(row)) % 4) + (zp + place(column)) % 4
 
             @pl.when(j <= diag)
@@ -589,13 +583,13 @@
 
             return c
 
-        lax.fori_loop(0, 2 * n - 1, one, 0)
-
-    def backward_shell(k):
-        shell(k, lambda j: backward(j, 0))
-
-    def finish_shell(k):
-        shell(k, sib_add)
+        lax.fori_loop(k if whole_column else k + 1, 4, one, 0)
+
+    def backward_shell(k, whole_column):
+        shell(k, whole_column, lambda j: backward(j, 0))
+
+    def finish_shell(k, whole_column):
+        shell(k, whole_column, sib_add)
 
     def remote(src, dst, sem, target, send=rs_send):
         return pltpu.make_async_remote_copy(
@@ -704,26 +698,33 @@
         f(0)
         f(1)
 
-    backward_shell(0)
-    finish_shell(0)
-    by_core(lambda: both(lambda w: x_half(w).start()), lambda: both(lambda w: z_half(w).start()))
+    def nothing():
+        pass
+
+    backward_shell(0, True)
     states_back()
-    backward_shell(1)
+    finish_shell(0, True)
+    by_core(nothing, lambda: both(lambda w: z_half(w).start()))
+    backward_shell(0, False)
+    finish_shell(0, False)
+    by_core(lambda: both(lambda w: x_half(w).start()), nothing)
     next(proj, None)
-    finish_shell(1)
-    by_core(lambda: x_next(0), lambda: z_next(0, 1))
-    backward_shell(2)
+    backward_shell(1, True)
     next(proj, None)
-    finish_shell(2)
-
-    def third():
-        z_next(1, 1)
-        z_next(0, 2)
-
-    by_core(lambda: x_next(1), third)
-    backward_shell(3)
+    finish_shell(1, True)
+    by_core(nothing, lambda: z_next(0, 1))
+    backward_shell(1, False)
+    backward_shell(2, True)
+    finish_shell(1, False)
+    finish_shell(2, True)
+    by_core(lambda: x_next(0), lambda: z_next(1, 1))
+    next(proj, None)
+    backward_shell(2, False)
+    backward_shell(3, True)
+    finish_shell(2, False)
+    by_core(lambda: x_next(1), lambda: z_next(0, 2))
     states_last()
-    finish_shell(3)
+    finish_shell(3, True)
     for g in range(GROUPS):
         dq_ref[:, g * 128:(g + 1) * 128] = (acc[:, g * 128:(g + 1) * 128] * SCALE).T.astype(BF16)
 
@@ -803,21 +804,18 @@
             yield
 
     final = states()
-    by_core(x_sum, lambda: z_next(1, 2))
+    by_core(nothing, lambda: z_next(1, 2))
+    next(proj, None)
+    by_core(x_sum, lambda: z_next(0, 3))
     next(final)
-    next(proj, None)
-    by_core(lambda: None, lambda: z_next(0, 3))
-    next(final)
-    by_core(lambda: None, lambda: z_next(1, 3))
+    by_core(nothing, lambda: z_next(1, 3))
     next(proj, None)
     for _ in final:
         pass
-    by_core(lambda: None, z_sum)
-    next(proj, None)
-    by_core(last_zero, last_one)
+    by_core(nothing, z_sum)
     for _ in proj:
         pass
-
+    by_core(last_zero, last_one)
     for ref in (kv.at[0, pl.ds(0, 3)], kv.at[0, 3, pl.ds(0, 7)]):
         pltpu.make_async_copy(ref, ref, rs_send).wait()
     for ref in (pj.at[0], pj.at[1, pl.ds(0, 7)]):

time: 98.4 us -> 95.3 us (0.968); the launches traced: 96.5 us -> 95.2 us
  Pallas kernels: 95.9 us -> 94.5 us
    pallas_call x1, Pallas kernels: 93.7 us -> 92.3 us  [per_device(): pl.pallas_call(kernel, out_shape=shapes, in_specs=[vm] * 4 + [pl.BlockSpe...]
where the time goes in v3:
time: 95.3 us; the launch traced here: 95.2 us
  Pallas kernels  94.5 us (99%)
    pallas_call x1, Pallas kernels, per_device(): pl.pallas_call(kernel, out_shape=shapes, in_specs=[vm] * 4 + [pl.BlockSpe...  92.3 us
    pallas_call x1, Pallas kernels, per_device(): pl.pallas_call(copy_kernel, out_shape=shapes, in_specs=[vm] * 7, out_spec...  2.2 us

profile of v3, /device:TPU:1, one launch (start us, length us, event | category | flops | bytes accessed | tf_op | source)
XLA Modules:
  0.0 95.2 jit_solution(10072531057314774129)
XLA Ops:
  0.6 92.3 %shard_map.153 = (bf16[128,640]{1,0:T(8,128)(2,1)}, bf16[128,128]{1,0:T(8,128)(2,1)}, bf16[128,128]{1,0:T(8,128)(2,1)}, f32[80,640]{1,0:T(8,128)}, bf16[128,1024...) custom-call(bf16[128,640]{1,0:T(8,128)(2,1)} %q_ref.1, bf16[128,128]{1,0:T(8,128)(2,1)} %k_ref.1, ...), custom_call_target="tpu_custom_call" | custom-call | tf_op jit(solution)/shard_map/pallas_call | solution.py:847
  93.0 2.2 %shard_map.154 = (bf16[128,640]{1,0:T(8,128)(2,1)}, bf16[128,128]{1,0:T(8,128)(2,1)}, bf16[128,128]{1,0:T(8,128)(2,1)}, f32[80,640]{1,0:T(8,128)}, bf16[128,1024...) custom-call(bf16[128,640]{1,0:T(8,128)(2,1)} %get-tuple-element.14.refs_0_, ...), custom_call_target="tpu_custom_call" | custom-call | tf_op jit(solution)/shard_map/pallas_call | solution.py:906
